TPU v7x, 32 devices: a whole 2x2x4 slice. The times are simulated.
32 devices in a mesh: env: 2 (over y), gx: 4 (over x, core), gy: 4 (over z).
Axes of the slice: x: 2, y: 2, z: 4, core: 2. Of those that a mesh axis runs over, the one named last changes fastest.
Arguments:
- old_state: float32 [1024, 3, 128, 128], P(('env', 'gx', 'gy')), parts along dimension 0, may hold values from -0.8 to 1.5, as said below
- bed: float32 [512, 128, 128], P(('env', 'gx', 'gy')), parts along dimension 0, may hold values from -0.5 to 0.5
- roughness: float32 [512, 128, 128], P(('env', 'gx', 'gy')), parts along dimension 0, may hold values from 0.02 to 0.2
- levels: int32 [512], P(('env', 'gx', 'gy')), parts along dimension 0, may hold values from 0 to 2
- sources: int32 [512], P('env'), parts along dimension 0, may hold values from 0 to 511, as said below
- neighbours: int32 [512, 8], P(('env', 'gx', 'gy')), parts along dimension 0, may hold values from -1 to 255, as said below
- face_codes: int32 [512, 4], P(('env', 'gx', 'gy')), parts along dimension 0, may hold values from 0 to 4, as said below
- step_index: int32 [6], P('env'), parts along dimension 0, may hold values from 4 to 6
Outputs:
- new_state: float32 [512, 3, 128, 128], P(('env', 'gx', 'gy')), parts along dimension 0
There are 2 independent parts, one for each index of `env`. A program takes and returns all parts, laid end to end along the dimension named above; each array names one. Nothing has to cross between parts.
Inputs may be any that keep to these rules, and one draw needn't show every extreme that they name: Patch g lies on device g // 16 of gx+gy (gx slowest) and takes old slot sources[g], held by device sources[g] // 32; that device has the same gy index and a gx index that differs by at most one. No old slot is used twice. From one device to the one beside it along gx, in each direction, at most 8 patches move, and exactly 8 for some pair in every draw. `neighbours`: entries 2f and 2f+1 name the patches beside face f, -1 for a wall. A named patch lies on the same device as patch g, or for face 0 on the device one lower along gx, face 1 one higher along gx, face 2 one lower along gy, face 3 one higher along gy. Entry 2f+1 equals entry 2f unless the face code is 3; then it lies on the same device as entry 2f. `face_codes`: 0: the patch beside has the same level; 1: it is coarser and this face meets the lower half of its face; 2: the upper half; 3: two finer patches (entry 2f along the lower half, 2f+1 along the upper); 4: a wall, both entries -1. `old_state`: component 0 lies in 0.5 to 1.5; components 1 and 2 in -0.8 to 0.8.
All inputs are finite; a program needn't handle non-finite values.
Results may differ from a plain program's by a relative error of at most 0.0003.
Values sent between devices are 32-bit elements; how exact they have to be, the bound alone decides.
A program may use at most 128 MiB of HBM per device.

v0:
```python
import jax
import jax.numpy as jnp
from jax import lax
from jax.sharding import PartitionSpec as P

STEPS = 3


GRAVITY = 9.81
COARSE_SPACING = 32.0
STEP_BASE = 0.15


def padded(value, sides, width):
    for axis, dim in sides:
        devices, length = (lax.axis_size(axis), value.shape[dim])
        up = [(i, (i + 1) % devices) for i in range(devices - 1)]
        down = [(j, i) for i, j in up]
        last = lax.slice_in_dim(value, length - width, length, axis=dim)
        first = lax.slice_in_dim(value, 0, width, axis=dim)
        before = lax.ppermute(last, axis, up)
        after = lax.ppermute(first, axis, down)
        value = jnp.concatenate([before, value, after], axis=dim)
    return value


def minmod(first_diff, second_diff):
    return (
        0.5
        * (jnp.sign(first_diff) + jnp.sign(second_diff))
        * jnp.minimum(jnp.abs(first_diff), jnp.abs(second_diff))
    )


def take_range(array, start, stop, axis):
    return lax.slice_in_dim(array, start, stop, axis=axis)


def strips_of(field):
    west = jnp.swapaxes(field[..., 0:4], -1, -2)
    east = jnp.swapaxes(jnp.flip(field[..., -4:], -1), -1, -2)
    south = field[..., 0:4, :]
    north = jnp.flip(field[..., -4:, :], -2)
    return jnp.stack([west, east, south, north], axis=1)


def combine(first, second, own, codes, signs):
    half = first.shape[-1] // 2
    same = first[..., 0:2, :]
    edge = first[..., 0, :]
    lower = jnp.repeat(edge[..., :half], 2, axis=-1)
    upper = jnp.repeat(edge[..., half:], 2, axis=-1)
    lower = jnp.stack([lower, lower], axis=-2)
    upper = jnp.stack([upper, upper], axis=-2)

    def pooled(strips):
        blocks = strips.reshape(strips.shape[:-2] + (2, 2, half, 2))
        return jnp.mean(blocks, axis=(-3, -1))

    finer = jnp.concatenate([pooled(first), pooled(second)], axis=-1)
    mirror = own[..., 0:2, :] * signs[None, :, :, None, None]
    code = codes[:, :, None, None, None]
    return jnp.where(
        code == 0,
        same,
        jnp.where(
            code == 1, lower, jnp.where(code == 2, upper, jnp.where(code == 3, finer, mirror))
        ),
    )


def pad_field(field, ghosts):
    west = jnp.swapaxes(jnp.flip(ghosts[:, 0], 2), -1, -2)
    east = jnp.swapaxes(ghosts[:, 1], -1, -2)
    south = jnp.flip(ghosts[:, 2], 2)
    north = ghosts[:, 3]
    along_x = jnp.concatenate([west, field, east], axis=-1)
    along_y = jnp.concatenate([south, field, north], axis=-2)
    return (along_x, along_y)


def sweep_axis(depth, normal, tangent, bed_padded, spacing, axis):
    length = depth.shape[axis] - 4

    def faces(values):
        diffs = take_range(values, 1, length + 4, axis) - take_range(values, 0, length + 3, axis)
        slopes = minmod(
            take_range(diffs, 0, length + 2, axis), take_range(diffs, 1, length + 3, axis)
        )
        left = take_range(values, 1, length + 2, axis) + 0.5 * take_range(
            slopes, 0, length + 1, axis
        )
        right = take_range(values, 2, length + 3, axis) - 0.5 * take_range(
            slopes, 1, length + 2, axis
        )
        return (left, right)

    depth_left, depth_right = faces(depth)
    normal_left, normal_right = faces(normal)
    tangent_left, tangent_right = faces(tangent)
    speed_left = normal_left / depth_left
    speed_right = normal_right / depth_right
    celerity_left = jnp.sqrt(GRAVITY * depth_left)
    celerity_right = jnp.sqrt(GRAVITY * depth_right)
    slowest = jnp.minimum(
        jnp.minimum(speed_left - celerity_left, speed_right - celerity_right), 0.0
    )
    fastest = jnp.maximum(
        jnp.maximum(speed_left + celerity_left, speed_right + celerity_right), 0.0
    )

    def hll_flux(flux_left, flux_right, value_left, value_right):
        return (
            fastest * flux_left
            - slowest * flux_right
            + fastest * slowest * (value_right - value_left)
        ) / (fastest - slowest)

    mass_flux = hll_flux(normal_left, normal_right, depth_left, depth_right)
    normal_flux = hll_flux(
        normal_left * speed_left + 0.5 * GRAVITY * depth_left * depth_left,
        normal_right * speed_right + 0.5 * GRAVITY * depth_right * depth_right,
        normal_left,
        normal_right,
    )
    tangent_flux = hll_flux(
        tangent_left * speed_left, tangent_right * speed_right, tangent_left, tangent_right
    )

    def divergence(flux):
        return (take_range(flux, 1, length + 1, axis) - take_range(flux, 0, length, axis)) / spacing

    centre_depth = take_range(depth, 2, length + 2, axis)
    bed_slope = (
        take_range(bed_padded, 3, length + 3, axis) - take_range(bed_padded, 1, length + 1, axis)
    ) / (2.0 * spacing)
    return (
        -divergence(mass_flux),
        -divergence(normal_flux) - GRAVITY * centre_depth * bed_slope,
        -divergence(tangent_flux),
    )


def tendency(field, ghosts, bed_x, bed_y, roughness, spacing):
    along_x, along_y = pad_field(field, ghosts)
    mass_x, east_x, north_x = sweep_axis(
        along_x[:, 0], along_x[:, 1], along_x[:, 2], bed_x, spacing, 2
    )
    mass_y, north_y, east_y = sweep_axis(
        along_y[:, 0], along_y[:, 2], along_y[:, 1], bed_y, spacing, 1
    )
    depth = field[:, 0]
    east_flow = field[:, 1]
    north_flow = field[:, 2]
    drag = (
        GRAVITY
        * roughness
        * roughness
        * jnp.sqrt(east_flow * east_flow + north_flow * north_flow)
        / depth ** (7.0 / 3.0)
    )
    return jnp.stack(
        [
            mass_x + mass_y,
            east_x + east_y - drag * east_flow,
            north_x + north_y - drag * north_flow,
        ],
        axis=1,
    )


def spacing_of(levels):
    return jnp.where(
        levels == 0, COARSE_SPACING, jnp.where(levels == 1, COARSE_SPACING / 2, COARSE_SPACING / 4)
    ).astype(jnp.float32)[:, None, None]


def on_device(old_state, bed, roughness, levels, sources, neighbours, face_codes, step_index):
    owned = levels.shape[0]
    capacity = old_state.shape[0]
    across = lax.axis_size("gy")
    x_index = lax.axis_index("gx")
    y_index = lax.axis_index("gy")
    device = x_index * across + y_index
    mine = lax.dynamic_slice_in_dim(sources, device * owned, owned)
    source_dev = mine // capacity
    extended = padded(old_state, (("gx", 0),), capacity)
    block_pos = (source_dev - device) // across + 1
    state = jnp.take(
        extended,
        jnp.clip(block_pos * capacity + mine - source_dev * capacity, 0, 3 * capacity - 1),
        axis=0,
    )
    opposite = jnp.array([1, 0, 3, 2], jnp.int32)
    first_target = neighbours[:, 0::2]
    second_target = neighbours[:, 1::2]
    flow_signs = jnp.array(
        [[1.0, -1.0, 1.0], [1.0, -1.0, 1.0], [1.0, 1.0, -1.0], [1.0, 1.0, -1.0]], jnp.float32
    )
    bed_signs = jnp.ones((4, 1), jnp.float32)

    def bundle_index(target):
        safe = jnp.maximum(target, 0)
        owner = safe // owned
        local_slot = safe % owned
        block = (owner // across - x_index + 1) * 3 + (owner % across - y_index + 1)
        return jnp.clip((block * owned + local_slot) * 4 + opposite[None, :], 0, 36 * owned - 1)

    bed_field = bed[:, None]
    bed_strips = strips_of(bed_field)
    bed_got = padded(bed_strips[None, None], (("gx", 0), ("gy", 1)), 1)
    bed_flat = bed_got.reshape((9 * owned * 4,) + bed_strips.shape[2:])
    bed_ghosts = combine(
        jnp.take(bed_flat, bundle_index(first_target), axis=0),
        jnp.take(bed_flat, bundle_index(second_target), axis=0),
        bed_strips,
        face_codes,
        bed_signs,
    )
    bed_x, bed_y = pad_field(bed_field, bed_ghosts)
    bed_x = bed_x[:, 0]
    bed_y = bed_y[:, 0]
    spacing = spacing_of(levels)

    def state_ghosts(field):
        strips = strips_of(field)
        got = padded(strips[None, None], (("gx", 0), ("gy", 1)), 1)
        flat = got.reshape((9 * owned * 4,) + strips.shape[2:])
        first_index = bundle_index(first_target)
        second_index = bundle_index(second_target)
        return combine(
            jnp.take(flat, first_index, axis=0),
            jnp.take(flat, second_index, axis=0),
            strips,
            face_codes,
            flow_signs,
        )

    def evolve(field, step_size):
        ghosts = state_ghosts(field)
        return field + step_size * tendency(field, ghosts, bed_x, bed_y, roughness, spacing)

    def one_step(step, current):
        step_size = STEP_BASE * (2.0 + step_index[step].astype(jnp.float32)) / 5.0
        sectioned = evolve(current, step_size)
        return 0.5 * current + 0.5 * evolve(sectioned, step_size)

    return lax.fori_loop(0, STEPS, one_step, state)


def solution(mesh):
    in_specs = (
        P(("env", "gx", "gy"), None, None, None),
        P(("env", "gx", "gy"), None, None),
        P(("env", "gx", "gy"), None, None),
        P(("env", "gx", "gy")),
        P("env"),
        P(("env", "gx", "gy"), None),
        P(("env", "gx", "gy"), None),
        P("env"),
    )
    out_specs = P(("env", "gx", "gy"), None, None, None)
    return jax.shard_map(
        on_device, mesh=mesh, in_specs=in_specs, out_specs=out_specs, check_vma=False
    )
```

profile of v0, /device:TPU:0, one launch (start us, length us, event | category | flops | bytes accessed | tf_op | source)
XLA Modules:
  0.0 971.7 jit_solution(10764028580528188436)
XLA Ops:
  6.3 6.0 copy.602
  29.5 6.7 copy.622
  71.3 14.3 %pad_maximum_fusion.10 = f32[96,3,128,128]{3,2,1,0:T(8,128)} fusion(f32[32,3,128,128]{3,2,1,0:T(8,128)} %collective-permute-done.9, f32[32,3,128,128]{3,2,1,0:T(8,128)} %param.16, f32[32,3,128,128]{3,2,1,0:T(8,128)} %collective-permute-done.8), kind=kLoop, calls=%fused_computation.337 | loop fusion | flops 9437184 | bytes 37748736 | tf_op jit(solution)/shard_map/concatenate | solution.py:23
  85.6 7.2 gather_fusion.4
  98.3 869.4 %while.17 = (s32[]{:T(128)}, f32[16,3,128,128]{2,0,3,1:T(8,128)}, s32[3]{0:T(128)}, s32[16,4]{0,1:T(4,128)}, s32[16,4]{0,1:T(4,128)S(1)}, /*index=5*/s32[]{:T(12...) while((s32[]{:T(128)}, f32[16,3,128,128]{2,0,3,1:T(8,128)}, ...), condition=%wide.region_7.10_spmd.clone, body=%wide.region_2.9_spmd.sunk.clone.sunk | while | flops 162996624 | bytes 466311552 | solution.py:248
  103.1 40.2 %collective-permute-start.1 = (f32[1,1,16,4,3,4,128]{6,2,5,4,3,1,0:T(8,128)S(1)}, f32[1,1,16,4,3,4,128]{6,2,5,4,3,1,0:T(8,128)S(1)}, u32[]{:S(2)}, u32[]{:S(2)}) collective-permute-start(f32[1,1,16,4,3,4,128]{6,2,5,4,3,1,0:T(8,128)S(1)} %get-tuple-element.806), channel_id=1, source_target_pairs={{0,4},{4,8},{8,12},{1,5},{5,9},{9,13},{2,6},{6,10},{10,14},{3,7},{... | collective-permute-start | bytes 1179656 | tf_op jit(solution)/shard_map/while/body/eval_jaxpr/ppermute | solution.py:21
  160.7 13.7 %collective-permute-done.3 = f32[3,1,16,4,3,4,128]{6,2,5,4,3,1,0:T(8,128)S(1)} collective-permute-done((f32[3,1,16,4,3,4,128]{6,2,5,4,3,1,0:T(8,128)}, f32[3,1,16,4,3,4,128]{6,2,5,4,3,1,0:T(8,128)S(1)}, u32[]{:S(2)}, u32[]{:S(2)}) %collective-permute-start.3) | collective-permute-done | bytes 1179680 | tf_op jit(solution)/shard_map/while/body/eval_jaxpr/ppermute | solution.py:21
  200.1 5.5 reduce_sum.100
  271.0 6.5 collective-permute-start.5
  288.4 19.4 %collective-permute-done.7 = f32[3,1,16,4,3,4,128]{6,2,5,4,3,1,0:T(8,128)} collective-permute-done((f32[3,1,16,4,3,4,128]{6,2,5,4,3,1,0:T(8,128)}, f32[3,1,16,4,3,4,128]{6,2,5,4,3,1,0:T(8,128)}, u32[]{:S(2)}, u32[]{:S(2)}) %collective-permute-start.7) | collective-permute-done | bytes 1179680 | tf_op jit(solution)/shard_map/while/body/eval_jaxpr/ppermute | solution.py:21
  307.8 5.7 collective-permute-done.6
  418.1 6.0 collective-permute-start.1
  439.1 14.2 %collective-permute-done.3 = f32[3,1,16,4,3,4,128]{6,2,5,4,3,1,0:T(8,128)S(1)} collective-permute-done((f32[3,1,16,4,3,4,128]{6,2,5,4,3,1,0:T(8,128)}, f32[3,1,16,4,3,4,128]{6,2,5,4,3,1,0:T(8,128)S(1)}, u32[]{:S(2)}, u32[]{:S(2)}) %collective-permute-start.3) | collective-permute-done | bytes 1179680 | tf_op jit(solution)/shard_map/while/body/eval_jaxpr/ppermute | solution.py:21
  478.9 5.5 reduce_sum.100
  514.2 5.6 add_divide_fusion.18
  550.0 6.0 collective-permute-start.5
  565.1 19.6 %collective-permute-done.7 = f32[3,1,16,4,3,4,128]{6,2,5,4,3,1,0:T(8,128)} collective-permute-done((f32[3,1,16,4,3,4,128]{6,2,5,4,3,1,0:T(8,128)}, f32[3,1,16,4,3,4,128]{6,2,5,4,3,1,0:T(8,128)}, u32[]{:S(2)}, u32[]{:S(2)}) %collective-permute-start.7) | collective-permute-done | bytes 1179680 | tf_op jit(solution)/shard_map/while/body/eval_jaxpr/ppermute | solution.py:21
  584.7 5.7 collective-permute-done.6
  671.5 5.6 add_divide_fusion.23
  694.9 6.0 collective-permute-start.1
  715.3 14.2 %collective-permute-done.3 = f32[3,1,16,4,3,4,128]{6,2,5,4,3,1,0:T(8,128)S(1)} collective-permute-done((f32[3,1,16,4,3,4,128]{6,2,5,4,3,1,0:T(8,128)}, f32[3,1,16,4,3,4,128]{6,2,5,4,3,1,0:T(8,128)S(1)}, u32[]{:S(2)}, u32[]{:S(2)}) %collective-permute-start.3) | collective-permute-done | bytes 1179680 | tf_op jit(solution)/shard_map/while/body/eval_jaxpr/ppermute | solution.py:21
  826.1 6.0 collective-permute-start.5
  841.3 19.6 %collective-permute-done.7 = f32[3,1,16,4,3,4,128]{6,2,5,4,3,1,0:T(8,128)} collective-permute-done((f32[3,1,16,4,3,4,128]{6,2,5,4,3,1,0:T(8,128)}, f32[3,1,16,4,3,4,128]{6,2,5,4,3,1,0:T(8,128)}, u32[]{:S(2)}, u32[]{:S(2)}) %collective-permute-start.7) | collective-permute-done | bytes 1179680 | tf_op jit(solution)/shard_map/while/body/eval_jaxpr/ppermute | solution.py:21
  860.9 5.7 collective-permute-done.6
  (691 shorter events, 718.4 us)
Async XLA Ops:
  0.0 71.3 %collective-permute-start.8 = (f32[32,3,128,128]{3,2,1,0:T(8,128)}, f32[32,3,128,128]{3,2,1,0:T(8,128)}, u32[]{:S(2)}, u32[]{:S(2)}) collective-permute-start(f32[32,3,128,128]{3,2,1,0:T(8,128)} %param.16), channel_id=1, source_target_pairs={{0,4},{4,8},{8,12},{1,5},{5,9},{9,13},{2,6},{6,10},{10,14},{3,7},{... | collective-permute-start | bytes 18874376 | tf_op jit(solution)/shard_map/ppermute | solution.py:21
  5.0 66.2 %collective-permute-start.9 = (f32[32,3,128,128]{3,2,1,0:T(8,128)}, f32[32,3,128,128]{3,2,1,0:T(8,128)}, u32[]{:S(2)}, u32[]{:S(2)}) collective-permute-start(f32[32,3,128,128]{3,2,1,0:T(8,128)} %param.16), channel_id=1, source_target_pairs={{4,0},{8,4},{12,8},{5,1},{9,5},{13,9},{6,2},{10,6},{14,10},{7,3},{... | collective-permute-start | bytes 18874376 | tf_op jit(solution)/shard_map/ppermute | solution.py:22
  16.7 22.4 %collective-permute-start.11 = (f32[1,1,16,4,1,4,128]{6,2,5,4,3,1,0:T(8,128)S(1)}, f32[1,1,16,4,1,4,128]{6,2,5,4,3,1,0:T(8,128)S(1)}, u32[]{:S(2)}, u32[]{:S(2)}) collective-permute-start(f32[1,1,16,4,1,4,128]{6,2,5,4,3,1,0:T(8,128)S(1)} %copy.606), channel_id=1, source_target_pairs={{4,0},{8,4},{12,8},{5,1},{9,5},{13,9},{6,2},{10,6},{14,10},{7,3},{... | collective-permute-start | bytes 393224 | tf_op jit(solution)/shard_map/ppermute | solution.py:22
  18.0 21.1 %collective-permute-start.10 = (f32[1,1,16,4,1,4,128]{6,2,5,4,3,1,0:T(8,128)S(1)}, f32[1,1,16,4,1,4,128]{6,2,5,4,3,1,0:T(8,128)S(1)}, u32[]{:S(2)}, u32[]{:S(2)}) collective-permute-start(f32[1,1,16,4,1,4,128]{6,2,5,4,3,1,0:T(8,128)S(1)} %copy.606), channel_id=1, source_target_pairs={{0,4},{4,8},{8,12},{1,5},{5,9},{9,13},{2,6},{6,10},{10,14},{3,7},{... | collective-permute-start | bytes 393224 | tf_op jit(solution)/shard_map/ppermute | solution.py:21
  39.1 10.1 %collective-permute-start.13 = (f32[3,1,16,4,1,4,128]{6,2,5,4,3,1,0:T(8,128)S(1)}, f32[3,1,16,4,1,4,128]{6,2,5,4,3,1,0:T(8,128)S(1)}, u32[]{:S(2)}, u32[]{:S(2)}) collective-permute-start(f32[3,1,16,4,1,4,128]{6,2,5,4,3,1,0:T(8,128)S(1)} %pad_maximum_fusion.13), channel_id=1, source_target_pairs={{1,0},{2,1},{3,2},{5,4},{6,5},{7,6},{9,8},{10,9},{11,10},{13,12},{... | collective-permute-start | bytes 1179656 | tf_op jit(solution)/shard_map/ppermute | solution.py:22
  40.4 10.2 %collective-permute-start.12 = (f32[3,1,16,4,1,4,128]{6,2,5,4,3,1,0:T(8,128)S(1)}, f32[3,1,16,4,1,4,128]{6,2,5,4,3,1,0:T(8,128)S(1)}, u32[]{:S(2)}, u32[]{:S(2)}) collective-permute-start(f32[3,1,16,4,1,4,128]{6,2,5,4,3,1,0:T(8,128)S(1)} %pad_maximum_fusion.13), channel_id=1, source_target_pairs={{0,1},{1,2},{2,3},{4,5},{5,6},{6,7},{8,9},{9,10},{10,11},{12,13},{... | collective-permute-start | bytes 1179656 | tf_op jit(solution)/shard_map/ppermute | solution.py:21
  103.1 41.5 %collective-permute-start.1 = (f32[1,1,16,4,3,4,128]{6,2,5,4,3,1,0:T(8,128)S(1)}, f32[1,1,16,4,3,4,128]{6,2,5,4,3,1,0:T(8,128)S(1)}, u32[]{:S(2)}, u32[]{:S(2)}) collective-permute-start(f32[1,1,16,4,3,4,128]{6,2,5,4,3,1,0:T(8,128)S(1)} %get-tuple-element.806), channel_id=1, source_target_pairs={{0,4},{4,8},{8,12},{1,5},{5,9},{9,13},{2,6},{6,10},{10,14},{3,7},{... | collective-permute-start | bytes 1179656 | tf_op jit(solution)/shard_map/while/body/eval_jaxpr/ppermute | solution.py:21
  148.4 26.0 %collective-permute-start.3 = (f32[3,1,16,4,3,4,128]{6,2,5,4,3,1,0:T(8,128)}, f32[3,1,16,4,3,4,128]{6,2,5,4,3,1,0:T(8,128)S(1)}, u32[]{:S(2)}, u32[]{:S(2)}) collective-permute-start(f32[3,1,16,4,3,4,128]{6,2,5,4,3,1,0:T(8,128)} %pad_maximum_fusion.22), channel_id=1, source_target_pairs={{0,1},{1,2},{2,3},{4,5},{5,6},{6,7},{8,9},{9,10},{10,11},{12,13},{... | collective-permute-start | bytes 3538952 | tf_op jit(solution)/shard_map/while/body/eval_jaxpr/ppermute | solution.py:21
  152.9 26.2 %collective-permute-start.2 = (f32[3,1,16,4,3,4,128]{6,2,5,4,3,1,0:T(8,128)}, f32[3,1,16,4,3,4,128]{6,2,5,4,3,1,0:T(8,128)S(1)}, u32[]{:S(2)}, u32[]{:S(2)}) collective-permute-start(f32[3,1,16,4,3,4,128]{6,2,5,4,3,1,0:T(8,128)} %pad_maximum_fusion.22), channel_id=1, source_target_pairs={{1,0},{2,1},{3,2},{5,4},{6,5},{7,6},{9,8},{10,9},{11,10},{13,12},{... | collective-permute-start | bytes 3538952 | tf_op jit(solution)/shard_map/while/body/eval_jaxpr/ppermute | solution.py:22
  271.0 7.9 collective-permute-start.5
  282.3 25.5 %collective-permute-start.7 = (f32[3,1,16,4,3,4,128]{6,2,5,4,3,1,0:T(8,128)}, f32[3,1,16,4,3,4,128]{6,2,5,4,3,1,0:T(8,128)}, u32[]{:S(2)}, u32[]{:S(2)}) collective-permute-start(f32[3,1,16,4,3,4,128]{6,2,5,4,3,1,0:T(8,128)} %pad_maximum_fusion.26), channel_id=1, source_target_pairs={{0,1},{1,2},{2,3},{4,5},{5,6},{6,7},{8,9},{9,10},{10,11},{12,13},{... | collective-permute-start | bytes 3538952 | tf_op jit(solution)/shard_map/while/body/eval_jaxpr/ppermute | solution.py:21
  286.7 26.8 %collective-permute-start.6 = (f32[3,1,16,4,3,4,128]{6,2,5,4,3,1,0:T(8,128)}, f32[3,1,16,4,3,4,128]{6,2,5,4,3,1,0:T(8,128)}, u32[]{:S(2)}, u32[]{:S(2)}) collective-permute-start(f32[3,1,16,4,3,4,128]{6,2,5,4,3,1,0:T(8,128)} %pad_maximum_fusion.26), channel_id=1, source_target_pairs={{1,0},{2,1},{3,2},{5,4},{6,5},{7,6},{9,8},{10,9},{11,10},{13,12},{... | collective-permute-start | bytes 3538952 | tf_op jit(solution)/shard_map/while/body/eval_jaxpr/ppermute | solution.py:22
  418.1 7.3 collective-permute-start.1
  428.8 24.6 %collective-permute-start.3 = (f32[3,1,16,4,3,4,128]{6,2,5,4,3,1,0:T(8,128)}, f32[3,1,16,4,3,4,128]{6,2,5,4,3,1,0:T(8,128)S(1)}, u32[]{:S(2)}, u32[]{:S(2)}) collective-permute-start(f32[3,1,16,4,3,4,128]{6,2,5,4,3,1,0:T(8,128)} %pad_maximum_fusion.22), channel_id=1, source_target_pairs={{0,1},{1,2},{2,3},{4,5},{5,6},{6,7},{8,9},{9,10},{10,11},{12,13},{... | collective-permute-start | bytes 3538952 | tf_op jit(solution)/shard_map/while/body/eval_jaxpr/ppermute | solution.py:21
  431.4 26.7 %collective-permute-start.2 = (f32[3,1,16,4,3,4,128]{6,2,5,4,3,1,0:T(8,128)}, f32[3,1,16,4,3,4,128]{6,2,5,4,3,1,0:T(8,128)S(1)}, u32[]{:S(2)}, u32[]{:S(2)}) collective-permute-start(f32[3,1,16,4,3,4,128]{6,2,5,4,3,1,0:T(8,128)} %pad_maximum_fusion.22), channel_id=1, source_target_pairs={{1,0},{2,1},{3,2},{5,4},{6,5},{7,6},{9,8},{10,9},{11,10},{13,12},{... | collective-permute-start | bytes 3538952 | tf_op jit(solution)/shard_map/while/body/eval_jaxpr/ppermute | solution.py:22
  550.0 7.3 collective-permute-start.5
  560.8 23.9 %collective-permute-start.7 = (f32[3,1,16,4,3,4,128]{6,2,5,4,3,1,0:T(8,128)}, f32[3,1,16,4,3,4,128]{6,2,5,4,3,1,0:T(8,128)}, u32[]{:S(2)}, u32[]{:S(2)}) collective-permute-start(f32[3,1,16,4,3,4,128]{6,2,5,4,3,1,0:T(8,128)} %pad_maximum_fusion.26), channel_id=1, source_target_pairs={{0,1},{1,2},{2,3},{4,5},{5,6},{6,7},{8,9},{9,10},{10,11},{12,13},{... | collective-permute-start | bytes 3538952 | tf_op jit(solution)/shard_map/while/body/eval_jaxpr/ppermute | solution.py:21
  563.6 26.8 %collective-permute-start.6 = (f32[3,1,16,4,3,4,128]{6,2,5,4,3,1,0:T(8,128)}, f32[3,1,16,4,3,4,128]{6,2,5,4,3,1,0:T(8,128)}, u32[]{:S(2)}, u32[]{:S(2)}) collective-permute-start(f32[3,1,16,4,3,4,128]{6,2,5,4,3,1,0:T(8,128)} %pad_maximum_fusion.26), channel_id=1, source_target_pairs={{1,0},{2,1},{3,2},{5,4},{6,5},{7,6},{9,8},{10,9},{11,10},{13,12},{... | collective-permute-start | bytes 3538952 | tf_op jit(solution)/shard_map/while/body/eval_jaxpr/ppermute | solution.py:22
  694.9 7.3 collective-permute-start.1
  705.7 23.8 %collective-permute-start.3 = (f32[3,1,16,4,3,4,128]{6,2,5,4,3,1,0:T(8,128)}, f32[3,1,16,4,3,4,128]{6,2,5,4,3,1,0:T(8,128)S(1)}, u32[]{:S(2)}, u32[]{:S(2)}) collective-permute-start(f32[3,1,16,4,3,4,128]{6,2,5,4,3,1,0:T(8,128)} %pad_maximum_fusion.22), channel_id=1, source_target_pairs={{0,1},{1,2},{2,3},{4,5},{5,6},{6,7},{8,9},{9,10},{10,11},{12,13},{... | collective-permute-start | bytes 3538952 | tf_op jit(solution)/shard_map/while/body/eval_jaxpr/ppermute | solution.py:21
  707.5 26.7 %collective-permute-start.2 = (f32[3,1,16,4,3,4,128]{6,2,5,4,3,1,0:T(8,128)}, f32[3,1,16,4,3,4,128]{6,2,5,4,3,1,0:T(8,128)S(1)}, u32[]{:S(2)}, u32[]{:S(2)}) collective-permute-start(f32[3,1,16,4,3,4,128]{6,2,5,4,3,1,0:T(8,128)} %pad_maximum_fusion.22), channel_id=1, source_target_pairs={{1,0},{2,1},{3,2},{5,4},{6,5},{7,6},{9,8},{10,9},{11,10},{13,12},{... | collective-permute-start | bytes 3538952 | tf_op jit(solution)/shard_map/while/body/eval_jaxpr/ppermute | solution.py:22
  826.1 7.3 collective-permute-start.5
  836.9 23.9 %collective-permute-start.7 = (f32[3,1,16,4,3,4,128]{6,2,5,4,3,1,0:T(8,128)}, f32[3,1,16,4,3,4,128]{6,2,5,4,3,1,0:T(8,128)}, u32[]{:S(2)}, u32[]{:S(2)}) collective-permute-start(f32[3,1,16,4,3,4,128]{6,2,5,4,3,1,0:T(8,128)} %pad_maximum_fusion.26), channel_id=1, source_target_pairs={{0,1},{1,2},{2,3},{4,5},{5,6},{6,7},{8,9},{9,10},{10,11},{12,13},{... | collective-permute-start | bytes 3538952 | tf_op jit(solution)/shard_map/while/body/eval_jaxpr/ppermute | solution.py:21
  839.8 26.8 %collective-permute-start.6 = (f32[3,1,16,4,3,4,128]{6,2,5,4,3,1,0:T(8,128)}, f32[3,1,16,4,3,4,128]{6,2,5,4,3,1,0:T(8,128)}, u32[]{:S(2)}, u32[]{:S(2)}) collective-permute-start(f32[3,1,16,4,3,4,128]{6,2,5,4,3,1,0:T(8,128)} %pad_maximum_fusion.26), channel_id=1, source_target_pairs={{1,0},{2,1},{3,2},{5,4},{6,5},{7,6},{9,8},{10,9},{11,10},{13,12},{... | collective-permute-start | bytes 3538952 | tf_op jit(solution)/shard_map/while/body/eval_jaxpr/ppermute | solution.py:22
  (111 other events, 793.4 us)
where the time goes:
time: 988 us; the launch traced here: 972 us
  other arithmetic  384 us (39%)
  local copies, waits for them, and re-layouts  305 us (31%)
  waiting for transfers between devices  150 us (15%)
  starting transfers between devices  124 us (13%)
    ppermute x15, starting transfers between devices, padded(): before = lax.ppermute(last, axis, up)  104 us
    ppermute x15, waiting for transfers between devices, padded(): before = lax.ppermute(last, axis, up)  102 us
    div x24, other arithmetic, hll_flux(): (fastest * flux_left - slowest * flux_right + fastest * slowest * (value_...  87.8 us
    reduce_sum x14, other arithmetic, pooled(): return jnp.mean(blocks, axis=(-3, -1))  64 us
    ppermute x15, waiting for transfers between devices, padded(): after = lax.ppermute(first, axis, down)  47.8 us
    mul x36, other arithmetic, minmod(): 0.5 * (jnp.sign(first_diff) + jnp.sign(second_diff))  33.5 us
    concatenate x6, other arithmetic, pad_field(): along_y = jnp.concatenate([south, field, north], axis=-2)  32 us
    another operation x12, other arithmetic, tendency(): jnp.stack([mass_x + mass_y, east_x + east_y - drag * east_flow, north_x +...  28.9 us
  transfers between devices with their start and end apart: 30, of which 20 were waited for; matrix products, arithmetic and copies ran while one was open for 7% of the time, Pallas kernels for 0%

commit v1 on v0

v1 whole, which is shorter than its diff:
```python
import functools

import jax
import jax.numpy as jnp
from jax import lax
from jax.experimental import pallas as pl
from jax.experimental.pallas import tpu as pltpu
from jax.sharding import PartitionSpec as P

STEPS = 3
MOVE = 8
GRAVITY = 9.81
COARSE_SPACING = 32.0
STEP_BASE = 0.15
VMEM_BYTES = 40 * 1024 * 1024
OPPOSITE = (1, 0, 3, 2)
FLIPPED = (1, 1, 2, 2)
LOW, HIGH = 8, 136


def minmod(a, b):
    return jnp.maximum(jnp.minimum(a, b), 0.0) + jnp.minimum(jnp.maximum(a, b), 0.0)


def fluxes(padded, flux, normal, tangent):
    for chunk in range(17):
        r = 8 * chunk

        def faces(q):
            v0, v1, v2, v3 = (padded[q, r + 6 + s : r + 14 + s, :] for s in range(4))
            a, b, c = v1 - v0, v2 - v1, v3 - v2
            return v1 + 0.5 * minmod(a, b), v2 - 0.5 * minmod(b, c)

        hl, hr = faces(0)
        nl, nr = faces(normal)
        tl, tr = faces(tangent)
        ul, ur = nl / hl, nr / hr
        gl, gr = GRAVITY * hl, GRAVITY * hr
        cl, cr = jnp.sqrt(gl), jnp.sqrt(gr)
        slow = jnp.minimum(jnp.minimum(ul - cl, ur - cr), 0.0)
        fast = jnp.maximum(jnp.maximum(ul + cl, ur + cr), 0.0)
        inv = 1.0 / (fast - slow)
        wl, wr, wd = fast * inv, slow * inv, fast * slow * inv
        flux[0, r : r + 8, :] = wl * nl - wr * nr + wd * (hr - hl)
        flux[1, r : r + 8, :] = (
            wl * (nl * ul + 0.5 * gl * hl) - wr * (nr * ur + 0.5 * gr * hr) + wd * (nr - nl)
        )
        flux[2, r : r + 8, :] = wl * (tl * ul) - wr * (tr * ur) + wd * (tr - tl)


def divergence(padded, flux, r):
    mass = flux[0, r + 1 : r + 9, :] - flux[0, r : r + 8, :]
    slope = padded[3, r + 9 : r + 17, :] - padded[3, r + 7 : r + 15, :]
    depth = padded[0, r + 8 : r + 16, :]
    normal = flux[1, r + 1 : r + 9, :] - flux[1, r : r + 8, :] + (0.5 * GRAVITY) * depth * slope
    tangent = flux[2, r + 1 : r + 9, :] - flux[2, r : r + 8, :]
    return mass, normal, tangent


def write_strips(fields, fields_t, strips):
    for c in range(4):
        for d in range(4):
            row = slice(4 * c + d, 4 * c + d + 1)
            strips[0][0, row, :] = fields_t(c, d)
            strips[1][0, row, :] = fields_t(c, 127 - d)
            strips[2][0, row, :] = fields(c, d)
            strips[3][0, row, :] = fields(c, 127 - d)


def write_ghosts(patch, ints, own, got, pads):
    lane = lax.broadcasted_iota(jnp.int32, (16, 128), 1)
    half = lane // 2
    even = (2 * lane) % 128
    low = lane < 64
    for f in range(4):
        opp = OPPOSITE[f]
        first = ints[0, 4 * patch + f]
        second = ints[1, 4 * patch + f]
        far = ints[2, 4 * patch + f] == 1
        code = ints[3, 4 * patch + f]
        a = jnp.where(far, got[f][first], own[opp][first])
        b = jnp.where(far, got[f][second], own[opp][second])
        index = jnp.where(
            code == 1, half, jnp.where(code == 2, half + 64, jnp.where(code == 3, even, lane))
        )
        take = functools.partial(jnp.take_along_axis, axis=1, mode="promise_in_bounds")
        a_even = take(a, index)
        odd = even + 1
        pair = jnp.where(low, a_even + take(a, odd), take(b, even) + take(b, odd))
        mine = own[f][patch]
        for c in range(4):
            for k in range(2):
                o = 4 * c + k
                same = a_even[o : o + 1]
                edge = a_even[4 * c : 4 * c + 1]
                p = 4 * c + 2 * k
                finer = 0.25 * (pair[p : p + 1] + pair[p + 1 : p + 2])
                mirror = mine[o : o + 1]
                if c == FLIPPED[f]:
                    mirror = -mirror
                value = jnp.where(
                    code == 0,
                    same,
                    jnp.where(code == 3, finer, jnp.where(code == 4, mirror, edge)),
                )
                row = (LOW - 1 - k) if f % 2 == 0 else (HIGH + k)
                pads[f // 2][c, row : row + 1, :] = value


def stage_kernel(second_stage, step, *refs):
    refs = list(refs)
    ints, floats = refs[0:2]
    state, state_t, bed, bed_t, rough = refs[2:7]
    at = 7
    base = None
    if second_stage:
        base = refs[7]
        at = 8
    own, got = refs[at : at + 4], refs[at + 4 : at + 8]
    at += 8
    last = second_stage and step == STEPS - 1
    out = refs[at]
    at += 1
    if not last:
        out_t, outs = refs[at], refs[at + 1 : at + 5]
        at += 5
    pad_x, pad_y, flux_x, flux_y, div_x = refs[at:]
    patch = pl.program_id(0)
    for c in range(3):
        pad_y[c, LOW:HIGH, :] = state[0, c]
        pad_x[c, LOW:HIGH, :] = state_t[0, c]
    pad_y[3, LOW:HIGH, :] = bed[0]
    pad_x[3, LOW:HIGH, :] = bed_t[0]
    write_ghosts(patch, ints, own, got, (pad_x, pad_y))
    fluxes(pad_x, flux_x, 1, 2)
    for chunk in range(16):
        r = 8 * chunk
        for q, value in enumerate(divergence(pad_x, flux_x, r)):
            div_x[q, r : r + 8, :] = value
    fluxes(pad_y, flux_y, 2, 1)
    for q in range(3):
        flux_x[q, 0:128, :] = div_x[q].T
    dt = floats[step]
    over = dt * floats[STEPS + patch]
    for chunk in range(16):
        r = 8 * chunk
        rows = slice(r, r + 8)
        mass, north, east = divergence(pad_y, flux_y, r)
        h, hu, hv = (state[0, c, rows, :] for c in range(3))
        n = rough[0, rows, :]
        drag = (dt * GRAVITY) * n * n * jnp.sqrt(hu * hu + hv * hv)
        drag = drag * jnp.exp((-7.0 / 3.0) * jnp.log(h))
        new = (
            h - over * (mass + flux_x[0, rows, :]),
            hu - over * (east + flux_x[1, rows, :]) - drag * hu,
            hv - over * (north + flux_x[2, rows, :]) - drag * hv,
        )
        for c in range(3):
            if second_stage:
                out[0, c, rows, :] = 0.5 * base[0, c, rows, :] + 0.5 * new[c]
            else:
                out[0, c, rows, :] = new[c]
    if not last:
        for c in range(3):
            out_t[0, c] = out[0, c].T
        write_strips(
            lambda c, d: out[0, c, d : d + 1, :] if c < 3 else bed[0, d : d + 1, :],
            lambda c, d: out_t[0, c, d : d + 1, :] if c < 3 else bed_t[0, d : d + 1, :],
            outs,
        )


def patch_spec(*shape):
    return pl.BlockSpec((1,) + shape, lambda i: (i,) + (0,) * len(shape))


def stage(second_stage, step, ints, floats, state, state_t, bed, bed_t, rough, base, own, got):
    owned = bed.shape[0]
    whole = pl.BlockSpec((owned, 16, 128), lambda i: (0, 0, 0))
    smem = pl.BlockSpec(memory_space=pltpu.SMEM)
    full, flat, strip = patch_spec(3, 128, 128), patch_spec(128, 128), patch_spec(16, 128)
    in_specs = [smem, smem, full, full, flat, flat, flat]
    args = [ints, floats, state, state_t, bed, bed_t, rough]
    if second_stage:
        in_specs.append(full)
        args.append(base)
    in_specs += [whole] * 8
    args += list(own) + list(got)
    field = jax.ShapeDtypeStruct(state.shape, jnp.float32)
    out_shape, out_specs = [field], [full]
    if not (second_stage and step == STEPS - 1):
        out_shape += [field] + [jax.ShapeDtypeStruct((owned, 16, 128), jnp.float32)] * 4
        out_specs += [full] + [strip] * 4
    scratch = [
        pltpu.VMEM((4, 152, 128), jnp.float32),
        pltpu.VMEM((4, 152, 128), jnp.float32),
        pltpu.VMEM((3, 136, 128), jnp.float32),
        pltpu.VMEM((3, 136, 128), jnp.float32),
        pltpu.VMEM((3, 128, 128), jnp.float32),
    ]
    got_out = pl.pallas_call(
        functools.partial(stage_kernel, second_stage, step),
        grid=(owned,),
        in_specs=in_specs,
        out_specs=out_specs,
        out_shape=out_shape,
        scratch_shapes=scratch,
        compiler_params=pltpu.CompilerParams(vmem_limit_bytes=VMEM_BYTES),
        name="stage",
    )(*args)
    if len(got_out) == 1:
        return got_out[0], None, None
    return got_out[0], got_out[1], got_out[2:]


def pick_patches(table, indices):
    count = indices.shape[0]

    def body(index_ref, source, out):
        out[...] = source[...]

    return pl.pallas_call(
        body,
        grid_spec=pltpu.PrefetchScalarGridSpec(
            num_scalar_prefetch=1,
            grid=(count,),
            in_specs=[pl.BlockSpec((1, 3, 128, 128), lambda i, ind: (ind[i], 0, 0, 0))],
            out_specs=pl.BlockSpec((1, 3, 128, 128), lambda i, ind: (i, 0, 0, 0)),
        ),
        out_shape=jax.ShapeDtypeStruct((count, 3, 128, 128), jnp.float32),
        name="pick",
    )(indices, table)


def assemble(picks, old_state, from_low, from_high, bed):
    owned = bed.shape[0]

    def body(picks_ref, here, low, high, bed_ref, state, state_t, bed_t, *strips):
        where = picks_ref[0, pl.program_id(0)]
        for c in range(3):
            value = jnp.where(where == 0, low[0, c], jnp.where(where == 2, high[0, c], here[0, c]))
            state[0, c] = value
            state_t[0, c] = value.T
        bed_t[0] = bed_ref[0].T
        write_strips(
            lambda c, d: state[0, c, d : d + 1, :] if c < 3 else bed_ref[0, d : d + 1, :],
            lambda c, d: state_t[0, c, d : d + 1, :] if c < 3 else bed_t[0, d : d + 1, :],
            strips,
        )

    def chosen(row):
        return pl.BlockSpec((1, 3, 128, 128), lambda i, ind: (ind[row, i], 0, 0, 0))

    def each(*shape):
        return pl.BlockSpec((1,) + shape, lambda i, ind: (i,) + (0,) * len(shape))

    field = jax.ShapeDtypeStruct((owned, 3, 128, 128), jnp.float32)
    strip = jax.ShapeDtypeStruct((owned, 16, 128), jnp.float32)
    out = pl.pallas_call(
        body,
        grid_spec=pltpu.PrefetchScalarGridSpec(
            num_scalar_prefetch=1,
            grid=(owned,),
            in_specs=[chosen(1), chosen(2), chosen(3), each(128, 128)],
            out_specs=[each(3, 128, 128), each(3, 128, 128), each(128, 128)] + [each(16, 128)] * 4,
        ),
        out_shape=[field, field, jax.ShapeDtypeStruct(bed.shape, jnp.float32)] + [strip] * 4,
        compiler_params=pltpu.CompilerParams(vmem_limit_bytes=VMEM_BYTES),
        name="assemble",
    )(picks, old_state, from_low, from_high, bed)
    return out[0], out[1], out[2], out[3:]


def shifted(value, axis, up):
    devices = lax.axis_size(axis)
    pairs = [(i, i + 1) for i in range(devices - 1)]
    return lax.ppermute(value, axis, pairs if up else [(j, i) for i, j in pairs])


def exchange(strips):
    return [
        shifted(strips[1], "gx", True),
        shifted(strips[0], "gx", False),
        shifted(strips[3], "gy", True),
        shifted(strips[2], "gy", False),
    ]


def on_device(old_state, bed, roughness, levels, sources, neighbours, face_codes, step_index):
    owned = levels.shape[0]
    capacity = old_state.shape[0]
    across = lax.axis_size("gy")
    device = lax.axis_index("gx") * across + lax.axis_index("gy")
    slots = jnp.arange(MOVE, dtype=jnp.int32)

    def ranks(mask):
        count = jnp.arange(owned)
        before = count[:, None] > count[None, :]
        return jnp.sum(jnp.where(before & mask[None, :], 1, 0), axis=1)

    def to_send(target):
        theirs = lax.dynamic_slice_in_dim(sources, target * owned, owned)
        mask = theirs // capacity == device
        hit = mask[None, :] & (ranks(mask)[None, :] == slots[:, None])
        return jnp.sum(jnp.where(hit, theirs % capacity, 0), axis=1)

    sends = jnp.concatenate([to_send(device + across), to_send(device - across)])
    picked = pick_patches(old_state, sends.astype(jnp.int32))
    from_low = shifted(picked[:MOVE], "gx", True)
    from_high = shifted(picked[MOVE:], "gx", False)

    mine = lax.dynamic_slice_in_dim(sources, device * owned, owned)
    source_dev = mine // capacity
    is_low = source_dev == device - across
    is_high = source_dev == device + across
    picks = jnp.stack(
        [
            jnp.where(is_low, 0, jnp.where(is_high, 2, 1)),
            jnp.where(is_low | is_high, 0, mine % capacity),
            jnp.where(is_low, jnp.minimum(ranks(is_low), MOVE - 1), 0),
            jnp.where(is_high, jnp.minimum(ranks(is_high), MOVE - 1), 0),
        ]
    ).astype(jnp.int32)
    state, state_t, bed_t, strips = assemble(picks, old_state, from_low, from_high, bed)

    first = jnp.maximum(neighbours[:, 0::2], 0)
    second = jnp.maximum(neighbours[:, 1::2], 0)
    far = jnp.where(first // owned != device, 1, 0)
    ints = jnp.stack(
        [(first % owned).reshape(-1), (second % owned).reshape(-1), far.reshape(-1),
         face_codes.reshape(-1)]
    ).astype(jnp.int32)
    spacing = jnp.where(
        levels == 0, COARSE_SPACING, jnp.where(levels == 1, COARSE_SPACING / 2, COARSE_SPACING / 4)
    ).astype(jnp.float32)
    step_sizes = STEP_BASE * (2.0 + step_index.astype(jnp.float32)) / 5.0
    floats = jnp.concatenate([step_sizes, 1.0 / spacing])

    for step in range(STEPS):
        base = state
        got = exchange(strips)
        section, section_t, strips = stage(
            False, step, ints, floats, state, state_t, bed, bed_t, roughness, None, strips, got
        )
        got = exchange(strips)
        state, state_t, strips = stage(
            True, step, ints, floats, section, section_t, bed, bed_t, roughness, base, strips, got
        )
    return state


def solution(mesh):
    in_specs = (
        P(("env", "gx", "gy"), None, None, None),
        P(("env", "gx", "gy"), None, None),
        P(("env", "gx", "gy"), None, None),
        P(("env", "gx", "gy")),
        P("env"),
        P(("env", "gx", "gy"), None),
        P(("env", "gx", "gy"), None),
        P("env"),
    )
    out_specs = P(("env", "gx", "gy"), None, None, None)
    return jax.shard_map(
        on_device, mesh=mesh, in_specs=in_specs, out_specs=out_specs, check_vma=False
    )
```

time: 988 us -> 252 us (0.26); the launches traced: 972 us -> 247 us
  other arithmetic: 384 us -> 4.11 us
  local copies, waits for them, and re-layouts: 305 us -> 20.2 us
  waiting for transfers between devices: 150 us -> 17.5 us
  Pallas kernels: 0 us -> 115 us
  starting transfers between devices: 124 us -> 89.5 us
    ppermute x30 -> x26, waiting for transfers between devices: 150 us -> 17.5 us  [shifted(): lax.ppermute(value, axis, pairs if up else [(j, i) for i, j in pairs])]
    pallas_call x0 -> x8, Pallas kernels: none -> 115 us  [the longest x6 97.1 us: stage(): pl.pallas_call(functools.partial(stage_kernel, second_stage, step), grid=...]
    div x38 -> x2, other arithmetic: 98.7 us -> 0.01 us  [the longest x1 0.01 us: on_device(): step_sizes = STEP_BASE * (2.0 + step_index.astype(jnp.float32)) / 5.0]
    concatenate x27 -> x2, other arithmetic: 67.3 us -> 0.73 us  [the longest x1 0.66 us: on_device(): jnp.concatenate([to_send(device + across), to_send(device - across)])]
    reduce_sum x14 -> x4, other arithmetic: 64 us -> 0.47 us  [the longest x2 0.24 us: to_send(): return jnp.sum(jnp.where(hit, theirs % capacity, 0), axis=1)]
    gather x23 -> x0, local copies, waits for them, and re-layouts: 56.4 us -> none  [the longest x12 27.4 us: state_ghosts(): jnp.take(flat, second_index, axis=0)]
    select_n x21 -> x3, other arithmetic: 39.3 us -> 1.17 us  [the longest x1 0.59 us: on_device(): first % owned]
    reshape x19 -> x0, local copies, waits for them, and re-layouts: 38.1 us -> none  [the longest x6 18.9 us: state_ghosts(): flat = got.reshape((9 * owned * 4,) + strips.shape[2:])]
  transfers between devices with their start and end apart: 30 -> 26, of which waited for: 20 -> 11; matrix products, arithmetic and copies ran while one was open for 7% -> 3% of each run, Pallas kernels for 0% -> 0%
where the time goes in v1:
time: 252 us; the launch traced here: 247 us
  Pallas kernels  115 us (46%)
  starting transfers between devices  89.5 us (36%)
  local copies, waits for them, and re-layouts  20.2 us (8%)
  waiting for transfers between devices  17.5 us (7%)
  other arithmetic  4.11 us (2%)
    pallas_call x6, Pallas kernels, stage(): pl.pallas_call(functools.partial(stage_kernel, second_stage, step), grid=...  97.1 us
    ppermute x26, starting transfers between devices, shifted(): lax.ppermute(value, axis, pairs if up else [(j, i) for i, j in pairs])  89.5 us
    ppermute x26, waiting for transfers between devices, shifted(): lax.ppermute(value, axis, pairs if up else [(j, i) for i, j in pairs])  17.5 us
    unnamed x29, local copies, waits for them, and re-layouts  12.6 us
    pallas_call x1, Pallas kernels, assemble(): pl.pallas_call(body, grid_spec=pltpu.PrefetchScalarGridSpec(num_scalar_pr...  11.1 us
    pallas_call x1, Pallas kernels, pick_patches(): pl.pallas_call(body, grid_spec=pltpu.PrefetchScalarGridSpec(num_scalar_pr...  7.19 us
  transfers between devices with their start and end apart: 26, of which 11 were waited for; matrix products, arithmetic and copies ran while one was open for 3% of the time, Pallas kernels for 0%

profile of v1, /device:TPU:0, one launch (start us, length us, event | category | flops | bytes accessed | tf_op | source)
XLA Modules:
  0.0 247.2 jit_solution(17905691756590247384)
XLA Ops:
  1.9 7.2 %pick.1 = f32[16,3,128,128]{3,2,1,0:T(8,128)} custom-call(s32[16]{0:T(128)} %pad_add_fusion.2.index_ref, f32[32,3,128,128]{3,2,1,0:T(8,128)} %here.1), custom_call_target="tpu_custom_call" | custom-call | tf_op jit(solution)/shard_map/pick/pallas_call | solution.py:222
  9.1 4.0 %fusion.13 = (f32[8,3,128,128]{3,2,1,0:T(8,128)}, f32[8,3,128,128]{3,2,1,0:T(8,128)}) fusion(f32[16,3,128,128]{3,2,1,0:T(8,128)} %pick.1), kind=kLoop, calls=%fused_computation.56 | loop fusion | bytes 6291456 | tf_op jit(solution)/shard_map/slice | solution.py:310
  14.4 7.5 %collective-permute-start = (f32[8,3,128,128]{3,2,1,0:T(8,128)}, f32[8,3,128,128]{3,2,1,0:T(8,128)}, u32[]{:S(2)}, u32[]{:S(2)}) collective-permute-start(f32[8,3,128,128]{3,2,1,0:T(8,128)} %get-tuple-element.87), channel_id=1, source_target_pairs={{0,4},{4,8},{8,12},{1,5},{5,9},{9,13},{2,6},{6,10},{10,14},{3,7},{... | collective-permute-start | bytes 4718600 | tf_op jit(solution)/shard_map/ppermute | solution.py:277
  24.1 11.1 %assemble.1 = (f32[16,3,128,128]{3,2,1,0:T(8,128)S(1)}, f32[16,3,128,128]{3,2,1,0:T(8,128)S(1)}, f32[16,128,128]{2,1,0:T(8,128)S(1)}, f32[16,16,128]{2,1,0:T(8,1...) custom-call(s32[4,16]{1,0:T(4,128)S(1)} %pad_add_fusion.1.picks_ref, ...), custom_call_target="tpu_custom_call" | custom-call | tf_op jit(solution)/shard_map/assemble/pallas_call | solution.py:259
  39.7 19.3 %collective-permute-start.2 = (f32[16,16,128]{2,1,0:T(8,128)S(1)}, f32[16,16,128]{2,1,0:T(8,128)}, u32[]{:S(2)}, u32[]{:S(2)}) collective-permute-start(f32[16,16,128]{2,1,0:T(8,128)S(1)} %get-tuple-element.46.refs_8_), channel_id=1, source_target_pairs={{0,4},{4,8},{8,12},{1,5},{5,9},{9,13},{2,6},{6,10},{10,14},{3,7},{... | collective-permute-start | bytes 393224 | tf_op jit(solution)/shard_map/ppermute | solution.py:277
  60.3 5.2 %collective-permute-start.4 = (f32[16,16,128]{2,1,0:T(8,128)}, f32[16,16,128]{2,1,0:T(8,128)}, u32[]{:S(2)}, u32[]{:S(2)}) collective-permute-start(f32[16,16,128]{2,1,0:T(8,128)} %get-tuple-element.48.refs_10_), channel_id=1, source_target_pairs={{0,1},{1,2},{2,3},{4,5},{5,6},{6,7},{8,9},{9,10},{10,11},{12,13},{... | collective-permute-start | bytes 393224 | tf_op jit(solution)/shard_map/ppermute | solution.py:277
  70.7 1.9 copy-done.3
  72.6 16.2 %stage.6 = (f32[16,3,128,128]{3,2,1,0:T(8,128)S(1)}, f32[16,3,128,128]{3,2,1,0:T(8,128)S(1)}, f32[16,16,128]{2,1,0:T(8,128)S(1)}, f32[16,16,128]{2,1,0:T(8,128)S...) custom-call(s32[4,64]{1,0:T(4,128)S(1)} %pad_add_fusion.refs_0_, f32[19]{0:T(128)S(1)} %pad_maximum_fusion.refs_1_, ...), custom_call_target="tpu_custom_call" | custom-call | tf_op jit(solution)/shard_map/stage/pallas_call | solution.py:201
  91.7 3.9 %collective-permute-start.6 = (f32[16,16,128]{2,1,0:T(8,128)S(1)}, f32[16,16,128]{2,1,0:T(8,128)S(1)}, u32[]{:S(2)}, u32[]{:S(2)}) collective-permute-start(f32[16,16,128]{2,1,0:T(8,128)S(1)} %get-tuple-element.52.refs_9_), channel_id=1, source_target_pairs={{0,4},{4,8},{8,12},{1,5},{5,9},{9,13},{2,6},{6,10},{10,14},{3,7},{... | collective-permute-start | bytes 393224 | tf_op jit(solution)/shard_map/ppermute | solution.py:277
  97.0 4.6 %collective-permute-start.8 = (f32[16,16,128]{2,1,0:T(8,128)S(1)}, f32[16,16,128]{2,1,0:T(8,128)S(1)}, u32[]{:S(2)}, u32[]{:S(2)}) collective-permute-start(f32[16,16,128]{2,1,0:T(8,128)S(1)} %get-tuple-element.54.refs_11_), channel_id=1, source_target_pairs={{0,1},{1,2},{2,3},{4,5},{5,6},{6,7},{8,9},{9,10},{10,11},{12,13},{... | collective-permute-start | bytes 393224 | tf_op jit(solution)/shard_map/ppermute | solution.py:277
  105.0 17.0 %stage.7 = (f32[16,3,128,128]{3,2,1,0:T(8,128)S(1)}, f32[16,3,128,128]{3,2,1,0:T(8,128)S(1)}, f32[16,16,128]{2,1,0:T(8,128)S(1)}, f32[16,16,128]{2,1,0:T(8,128)S...) custom-call(s32[4,64]{1,0:T(4,128)S(1)} %pad_add_fusion.refs_0_, f32[19]{0:T(128)S(1)} %pad_maximum_fusion.refs_1_, ...), custom_call_target="tpu_custom_call" | custom-call | tf_op jit(solution)/shard_map/stage/pallas_call | solution.py:201
  124.9 3.1 %collective-permute-start.10 = (f32[16,16,128]{2,1,0:T(8,128)S(1)}, f32[16,16,128]{2,1,0:T(8,128)S(1)}, u32[]{:S(2)}, u32[]{:S(2)}) collective-permute-start(f32[16,16,128]{2,1,0:T(8,128)S(1)} %get-tuple-element.58.refs_8_), channel_id=1, source_target_pairs={{0,4},{4,8},{8,12},{1,5},{5,9},{9,13},{2,6},{6,10},{10,14},{3,7},{... | collective-permute-start | bytes 393224 | tf_op jit(solution)/shard_map/ppermute | solution.py:277
  129.3 5.0 %collective-permute-start.12 = (f32[16,16,128]{2,1,0:T(8,128)S(1)}, f32[16,16,128]{2,1,0:T(8,128)S(1)}, u32[]{:S(2)}, u32[]{:S(2)}) collective-permute-start(f32[16,16,128]{2,1,0:T(8,128)S(1)} %get-tuple-element.60.refs_10_), channel_id=1, source_target_pairs={{0,1},{1,2},{2,3},{4,5},{5,6},{6,7},{8,9},{9,10},{10,11},{12,13},{... | collective-permute-start | bytes 393224 | tf_op jit(solution)/shard_map/ppermute | solution.py:277
  136.0 1.8 collective-permute-done.12.refs_13_
  137.8 15.7 %stage.8 = (f32[16,3,128,128]{3,2,1,0:T(8,128)S(1)}, f32[16,3,128,128]{3,2,1,0:T(8,128)S(1)}, f32[16,16,128]{2,1,0:T(8,128)S(1)}, f32[16,16,128]{2,1,0:T(8,128)S...) custom-call(s32[4,64]{1,0:T(4,128)S(1)} %pad_add_fusion.refs_0_, f32[19]{0:T(128)S(1)} %pad_maximum_fusion.refs_1_, ...), custom_call_target="tpu_custom_call" | custom-call | tf_op jit(solution)/shard_map/stage/pallas_call | solution.py:201
  156.5 3.1 %collective-permute-start.14 = (f32[16,16,128]{2,1,0:T(8,128)S(1)}, f32[16,16,128]{2,1,0:T(8,128)S(1)}, u32[]{:S(2)}, u32[]{:S(2)}) collective-permute-start(f32[16,16,128]{2,1,0:T(8,128)S(1)} %get-tuple-element.64.refs_9_), channel_id=1, source_target_pairs={{0,4},{4,8},{8,12},{1,5},{5,9},{9,13},{2,6},{6,10},{10,14},{3,7},{... | collective-permute-start | bytes 393224 | tf_op jit(solution)/shard_map/ppermute | solution.py:277
  160.8 5.0 %collective-permute-start.16 = (f32[16,16,128]{2,1,0:T(8,128)S(1)}, f32[16,16,128]{2,1,0:T(8,128)S(1)}, u32[]{:S(2)}, u32[]{:S(2)}) collective-permute-start(f32[16,16,128]{2,1,0:T(8,128)S(1)} %get-tuple-element.66.refs_11_), channel_id=1, source_target_pairs={{0,1},{1,2},{2,3},{4,5},{5,6},{6,7},{8,9},{9,10},{10,11},{12,13},{... | collective-permute-start | bytes 393224 | tf_op jit(solution)/shard_map/ppermute | solution.py:277
  169.3 17.0 %stage.9 = (f32[16,3,128,128]{3,2,1,0:T(8,128)S(1)}, f32[16,3,128,128]{3,2,1,0:T(8,128)S(1)}, f32[16,16,128]{2,1,0:T(8,128)S(1)}, f32[16,16,128]{2,1,0:T(8,128)S...) custom-call(s32[4,64]{1,0:T(4,128)S(1)} %pad_add_fusion.refs_0_, f32[19]{0:T(128)S(1)} %pad_maximum_fusion.refs_1_, ...), custom_call_target="tpu_custom_call" | custom-call | tf_op jit(solution)/shard_map/stage/pallas_call | solution.py:201
  189.2 3.1 %collective-permute-start.18 = (f32[16,16,128]{2,1,0:T(8,128)S(1)}, f32[16,16,128]{2,1,0:T(8,128)S(1)}, u32[]{:S(2)}, u32[]{:S(2)}) collective-permute-start(f32[16,16,128]{2,1,0:T(8,128)S(1)} %get-tuple-element.70.refs_8_), channel_id=1, source_target_pairs={{0,4},{4,8},{8,12},{1,5},{5,9},{9,13},{2,6},{6,10},{10,14},{3,7},{... | collective-permute-start | bytes 393224 | tf_op jit(solution)/shard_map/ppermute | solution.py:277
  193.6 5.0 %collective-permute-start.20 = (f32[16,16,128]{2,1,0:T(8,128)S(1)}, f32[16,16,128]{2,1,0:T(8,128)S(1)}, u32[]{:S(2)}, u32[]{:S(2)}) collective-permute-start(f32[16,16,128]{2,1,0:T(8,128)S(1)} %get-tuple-element.72.refs_10_), channel_id=1, source_target_pairs={{0,1},{1,2},{2,3},{4,5},{5,6},{6,7},{8,9},{9,10},{10,11},{12,13},{... | collective-permute-start | bytes 393224 | tf_op jit(solution)/shard_map/ppermute | solution.py:277
  202.0 15.7 %stage.10 = (f32[16,3,128,128]{3,2,1,0:T(8,128)S(1)}, f32[16,3,128,128]{3,2,1,0:T(8,128)S(1)}, f32[16,16,128]{2,1,0:T(8,128)S(1)}, f32[16,16,128]{2,1,0:T(8,128)...) custom-call(s32[4,64]{1,0:T(4,128)S(1)} %pad_add_fusion.refs_0_, f32[19]{0:T(128)S(1)} %pad_maximum_fusion.refs_1_, ...), custom_call_target="tpu_custom_call" | custom-call | tf_op jit(solution)/shard_map/stage/pallas_call | solution.py:201
  219.0 3.1 %collective-permute-start.22 = (f32[16,16,128]{2,1,0:T(8,128)S(1)}, f32[16,16,128]{2,1,0:T(8,128)S(1)}, u32[]{:S(2)}, u32[]{:S(2)}) collective-permute-start(f32[16,16,128]{2,1,0:T(8,128)S(1)} %get-tuple-element.76.refs_9_), channel_id=1, source_target_pairs={{0,4},{4,8},{8,12},{1,5},{5,9},{9,13},{2,6},{6,10},{10,14},{3,7},{... | collective-permute-start | bytes 393224 | tf_op jit(solution)/shard_map/ppermute | solution.py:277
  223.5 5.0 %collective-permute-start.24 = (f32[16,16,128]{2,1,0:T(8,128)S(1)}, f32[16,16,128]{2,1,0:T(8,128)S(1)}, u32[]{:S(2)}, u32[]{:S(2)}) collective-permute-start(f32[16,16,128]{2,1,0:T(8,128)S(1)} %get-tuple-element.78.refs_11_), channel_id=1, source_target_pairs={{0,1},{1,2},{2,3},{4,5},{5,6},{6,7},{8,9},{9,10},{10,11},{12,13},{... | collective-permute-start | bytes 393224 | tf_op jit(solution)/shard_map/ppermute | solution.py:277
  231.7 15.5 %stage.11 = f32[16,3,128,128]{3,2,1,0:T(8,128)} custom-call(s32[4,64]{1,0:T(4,128)S(1)} %pad_add_fusion.refs_0_, f32[19]{0:T(128)S(1)} %pad_maximum_fusion.refs_1_, f32[16,3,128,128]{3,2,1,0:T(8,128)S(1)} %get-tuple-element.73.refs_2_, f32[16,3,128,128]{3,2,1,0:T(8,128)S(1)} %get-tuple-element.74.refs_3_, f32[16,128,128]{2,1,0:T(8,128)S(1)} %copy-done, ...), custom_call_target="tpu_custom_call" | custom-call | tf_op jit(solution)/shard_map/stage/pallas_call | solution.py:201
  (91 shorter events, 50.9 us)
Async XLA Ops:
  13.1 10.3 %collective-permute-start.1 = (f32[8,3,128,128]{3,2,1,0:T(8,128)}, f32[8,3,128,128]{3,2,1,0:T(8,128)}, u32[]{:S(2)}, u32[]{:S(2)}) collective-permute-start(f32[8,3,128,128]{3,2,1,0:T(8,128)} %get-tuple-element.86), channel_id=1, source_target_pairs={{4,0},{8,4},{12,8},{5,1},{9,5},{13,9},{6,2},{10,6},{14,10},{7,3},{... | collective-permute-start | bytes 4718600 | tf_op jit(solution)/shard_map/ppermute | solution.py:277
  14.4 9.7 %collective-permute-start = (f32[8,3,128,128]{3,2,1,0:T(8,128)}, f32[8,3,128,128]{3,2,1,0:T(8,128)}, u32[]{:S(2)}, u32[]{:S(2)}) collective-permute-start(f32[8,3,128,128]{3,2,1,0:T(8,128)} %get-tuple-element.87), channel_id=1, source_target_pairs={{0,4},{4,8},{8,12},{1,5},{5,9},{9,13},{2,6},{6,10},{10,14},{3,7},{... | collective-permute-start | bytes 4718600 | tf_op jit(solution)/shard_map/ppermute | solution.py:277
  38.4 32.2 %collective-permute-start.3 = (f32[16,16,128]{2,1,0:T(8,128)S(1)}, f32[16,16,128]{2,1,0:T(8,128)}, u32[]{:S(2)}, u32[]{:S(2)}) collective-permute-start(f32[16,16,128]{2,1,0:T(8,128)S(1)} %get-tuple-element.45.refs_7_), channel_id=1, source_target_pairs={{4,0},{8,4},{12,8},{5,1},{9,5},{13,9},{6,2},{10,6},{14,10},{7,3},{... | collective-permute-start | bytes 393224 | tf_op jit(solution)/shard_map/ppermute | solution.py:277
  39.7 31.0 %collective-permute-start.2 = (f32[16,16,128]{2,1,0:T(8,128)S(1)}, f32[16,16,128]{2,1,0:T(8,128)}, u32[]{:S(2)}, u32[]{:S(2)}) collective-permute-start(f32[16,16,128]{2,1,0:T(8,128)S(1)} %get-tuple-element.46.refs_8_), channel_id=1, source_target_pairs={{0,4},{4,8},{8,12},{1,5},{5,9},{9,13},{2,6},{6,10},{10,14},{3,7},{... | collective-permute-start | bytes 393224 | tf_op jit(solution)/shard_map/ppermute | solution.py:277
  59.1 11.6 %collective-permute-start.5 = (f32[16,16,128]{2,1,0:T(8,128)S(1)}, f32[16,16,128]{2,1,0:T(8,128)}, u32[]{:S(2)}, u32[]{:S(2)}) collective-permute-start(f32[16,16,128]{2,1,0:T(8,128)S(1)} %get-tuple-element.47.refs_9_), channel_id=1, source_target_pairs={{1,0},{2,1},{3,2},{5,4},{6,5},{7,6},{9,8},{10,9},{11,10},{13,12},{... | collective-permute-start | bytes 393224 | tf_op jit(solution)/shard_map/ppermute | solution.py:277
  60.3 10.4 %collective-permute-start.4 = (f32[16,16,128]{2,1,0:T(8,128)}, f32[16,16,128]{2,1,0:T(8,128)}, u32[]{:S(2)}, u32[]{:S(2)}) collective-permute-start(f32[16,16,128]{2,1,0:T(8,128)} %get-tuple-element.48.refs_10_), channel_id=1, source_target_pairs={{0,1},{1,2},{2,3},{4,5},{5,6},{6,7},{8,9},{9,10},{10,11},{12,13},{... | collective-permute-start | bytes 393224 | tf_op jit(solution)/shard_map/ppermute | solution.py:277
  90.4 11.1 %collective-permute-start.7 = (f32[16,16,128]{2,1,0:T(8,128)S(1)}, f32[16,16,128]{2,1,0:T(8,128)S(1)}, u32[]{:S(2)}, u32[]{:S(2)}) collective-permute-start(f32[16,16,128]{2,1,0:T(8,128)S(1)} %get-tuple-element.51.refs_8_), channel_id=1, source_target_pairs={{4,0},{8,4},{12,8},{5,1},{9,5},{13,9},{6,2},{10,6},{14,10},{7,3},{... | collective-permute-start | bytes 393224 | tf_op jit(solution)/shard_map/ppermute | solution.py:277
  91.7 9.8 %collective-permute-start.6 = (f32[16,16,128]{2,1,0:T(8,128)S(1)}, f32[16,16,128]{2,1,0:T(8,128)S(1)}, u32[]{:S(2)}, u32[]{:S(2)}) collective-permute-start(f32[16,16,128]{2,1,0:T(8,128)S(1)} %get-tuple-element.52.refs_9_), channel_id=1, source_target_pairs={{0,4},{4,8},{8,12},{1,5},{5,9},{9,13},{2,6},{6,10},{10,14},{3,7},{... | collective-permute-start | bytes 393224 | tf_op jit(solution)/shard_map/ppermute | solution.py:277
  97.0 8.0 %collective-permute-start.8 = (f32[16,16,128]{2,1,0:T(8,128)S(1)}, f32[16,16,128]{2,1,0:T(8,128)S(1)}, u32[]{:S(2)}, u32[]{:S(2)}) collective-permute-start(f32[16,16,128]{2,1,0:T(8,128)S(1)} %get-tuple-element.54.refs_11_), channel_id=1, source_target_pairs={{0,1},{1,2},{2,3},{4,5},{5,6},{6,7},{8,9},{9,10},{10,11},{12,13},{... | collective-permute-start | bytes 393224 | tf_op jit(solution)/shard_map/ppermute | solution.py:277
  123.6 10.7 %collective-permute-start.11 = (f32[16,16,128]{2,1,0:T(8,128)S(1)}, f32[16,16,128]{2,1,0:T(8,128)S(1)}, u32[]{:S(2)}, u32[]{:S(2)}) collective-permute-start(f32[16,16,128]{2,1,0:T(8,128)S(1)} %get-tuple-element.57.refs_7_), channel_id=1, source_target_pairs={{4,0},{8,4},{12,8},{5,1},{9,5},{13,9},{6,2},{10,6},{14,10},{7,3},{... | collective-permute-start | bytes 393224 | tf_op jit(solution)/shard_map/ppermute | solution.py:277
  124.9 9.4 %collective-permute-start.10 = (f32[16,16,128]{2,1,0:T(8,128)S(1)}, f32[16,16,128]{2,1,0:T(8,128)S(1)}, u32[]{:S(2)}, u32[]{:S(2)}) collective-permute-start(f32[16,16,128]{2,1,0:T(8,128)S(1)} %get-tuple-element.58.refs_8_), channel_id=1, source_target_pairs={{0,4},{4,8},{8,12},{1,5},{5,9},{9,13},{2,6},{6,10},{10,14},{3,7},{... | collective-permute-start | bytes 393224 | tf_op jit(solution)/shard_map/ppermute | solution.py:277
  128.0 8.0 %collective-permute-start.13 = (f32[16,16,128]{2,1,0:T(8,128)S(1)}, f32[16,16,128]{2,1,0:T(8,128)S(1)}, u32[]{:S(2)}, u32[]{:S(2)}) collective-permute-start(f32[16,16,128]{2,1,0:T(8,128)S(1)} %get-tuple-element.59.refs_9_), channel_id=1, source_target_pairs={{1,0},{2,1},{3,2},{5,4},{6,5},{7,6},{9,8},{10,9},{11,10},{13,12},{... | collective-permute-start | bytes 393224 | tf_op jit(solution)/shard_map/ppermute | solution.py:277
  129.3 8.5 %collective-permute-start.12 = (f32[16,16,128]{2,1,0:T(8,128)S(1)}, f32[16,16,128]{2,1,0:T(8,128)S(1)}, u32[]{:S(2)}, u32[]{:S(2)}) collective-permute-start(f32[16,16,128]{2,1,0:T(8,128)S(1)} %get-tuple-element.60.refs_10_), channel_id=1, source_target_pairs={{0,1},{1,2},{2,3},{4,5},{5,6},{6,7},{8,9},{9,10},{10,11},{12,13},{... | collective-permute-start | bytes 393224 | tf_op jit(solution)/shard_map/ppermute | solution.py:277
  155.2 10.7 %collective-permute-start.15 = (f32[16,16,128]{2,1,0:T(8,128)S(1)}, f32[16,16,128]{2,1,0:T(8,128)S(1)}, u32[]{:S(2)}, u32[]{:S(2)}) collective-permute-start(f32[16,16,128]{2,1,0:T(8,128)S(1)} %get-tuple-element.63.refs_8_), channel_id=1, source_target_pairs={{4,0},{8,4},{12,8},{5,1},{9,5},{13,9},{6,2},{10,6},{14,10},{7,3},{... | collective-permute-start | bytes 393224 | tf_op jit(solution)/shard_map/ppermute | solution.py:277
  156.5 9.4 %collective-permute-start.14 = (f32[16,16,128]{2,1,0:T(8,128)S(1)}, f32[16,16,128]{2,1,0:T(8,128)S(1)}, u32[]{:S(2)}, u32[]{:S(2)}) collective-permute-start(f32[16,16,128]{2,1,0:T(8,128)S(1)} %get-tuple-element.64.refs_9_), channel_id=1, source_target_pairs={{0,4},{4,8},{8,12},{1,5},{5,9},{9,13},{2,6},{6,10},{10,14},{3,7},{... | collective-permute-start | bytes 393224 | tf_op jit(solution)/shard_map/ppermute | solution.py:277
  159.5 8.0 %collective-permute-start.17 = (f32[16,16,128]{2,1,0:T(8,128)S(1)}, f32[16,16,128]{2,1,0:T(8,128)S(1)}, u32[]{:S(2)}, u32[]{:S(2)}) collective-permute-start(f32[16,16,128]{2,1,0:T(8,128)S(1)} %get-tuple-element.65.refs_10_), channel_id=1, source_target_pairs={{1,0},{2,1},{3,2},{5,4},{6,5},{7,6},{9,8},{10,9},{11,10},{13,12},{... | collective-permute-start | bytes 393224 | tf_op jit(solution)/shard_map/ppermute | solution.py:277
  160.8 8.4 %collective-permute-start.16 = (f32[16,16,128]{2,1,0:T(8,128)S(1)}, f32[16,16,128]{2,1,0:T(8,128)S(1)}, u32[]{:S(2)}, u32[]{:S(2)}) collective-permute-start(f32[16,16,128]{2,1,0:T(8,128)S(1)} %get-tuple-element.66.refs_11_), channel_id=1, source_target_pairs={{0,1},{1,2},{2,3},{4,5},{5,6},{6,7},{8,9},{9,10},{10,11},{12,13},{... | collective-permute-start | bytes 393224 | tf_op jit(solution)/shard_map/ppermute | solution.py:277
  187.9 10.7 %collective-permute-start.19 = (f32[16,16,128]{2,1,0:T(8,128)S(1)}, f32[16,16,128]{2,1,0:T(8,128)S(1)}, u32[]{:S(2)}, u32[]{:S(2)}) collective-permute-start(f32[16,16,128]{2,1,0:T(8,128)S(1)} %get-tuple-element.69.refs_7_), channel_id=1, source_target_pairs={{4,0},{8,4},{12,8},{5,1},{9,5},{13,9},{6,2},{10,6},{14,10},{7,3},{... | collective-permute-start | bytes 393224 | tf_op jit(solution)/shard_map/ppermute | solution.py:277
  189.2 9.4 %collective-permute-start.18 = (f32[16,16,128]{2,1,0:T(8,128)S(1)}, f32[16,16,128]{2,1,0:T(8,128)S(1)}, u32[]{:S(2)}, u32[]{:S(2)}) collective-permute-start(f32[16,16,128]{2,1,0:T(8,128)S(1)} %get-tuple-element.70.refs_8_), channel_id=1, source_target_pairs={{0,4},{4,8},{8,12},{1,5},{5,9},{9,13},{2,6},{6,10},{10,14},{3,7},{... | collective-permute-start | bytes 393224 | tf_op jit(solution)/shard_map/ppermute | solution.py:277
  192.3 7.9 %collective-permute-start.21 = (f32[16,16,128]{2,1,0:T(8,128)S(1)}, f32[16,16,128]{2,1,0:T(8,128)S(1)}, u32[]{:S(2)}, u32[]{:S(2)}) collective-permute-start(f32[16,16,128]{2,1,0:T(8,128)S(1)} %get-tuple-element.71.refs_9_), channel_id=1, source_target_pairs={{1,0},{2,1},{3,2},{5,4},{6,5},{7,6},{9,8},{10,9},{11,10},{13,12},{... | collective-permute-start | bytes 393224 | tf_op jit(solution)/shard_map/ppermute | solution.py:277
  193.6 8.4 %collective-permute-start.20 = (f32[16,16,128]{2,1,0:T(8,128)S(1)}, f32[16,16,128]{2,1,0:T(8,128)S(1)}, u32[]{:S(2)}, u32[]{:S(2)}) collective-permute-start(f32[16,16,128]{2,1,0:T(8,128)S(1)} %get-tuple-element.72.refs_10_), channel_id=1, source_target_pairs={{0,1},{1,2},{2,3},{4,5},{5,6},{6,7},{8,9},{9,10},{10,11},{12,13},{... | collective-permute-start | bytes 393224 | tf_op jit(solution)/shard_map/ppermute | solution.py:277
  217.7 10.7 %collective-permute-start.23 = (f32[16,16,128]{2,1,0:T(8,128)S(1)}, f32[16,16,128]{2,1,0:T(8,128)S(1)}, u32[]{:S(2)}, u32[]{:S(2)}) collective-permute-start(f32[16,16,128]{2,1,0:T(8,128)S(1)} %get-tuple-element.75.refs_8_), channel_id=1, source_target_pairs={{4,0},{8,4},{12,8},{5,1},{9,5},{13,9},{6,2},{10,6},{14,10},{7,3},{... | collective-permute-start | bytes 393224 | tf_op jit(solution)/shard_map/ppermute | solution.py:277
  219.0 9.4 %collective-permute-start.22 = (f32[16,16,128]{2,1,0:T(8,128)S(1)}, f32[16,16,128]{2,1,0:T(8,128)S(1)}, u32[]{:S(2)}, u32[]{:S(2)}) collective-permute-start(f32[16,16,128]{2,1,0:T(8,128)S(1)} %get-tuple-element.76.refs_9_), channel_id=1, source_target_pairs={{0,4},{4,8},{8,12},{1,5},{5,9},{9,13},{2,6},{6,10},{10,14},{3,7},{... | collective-permute-start | bytes 393224 | tf_op jit(solution)/shard_map/ppermute | solution.py:277
  223.5 8.2 %collective-permute-start.24 = (f32[16,16,128]{2,1,0:T(8,128)S(1)}, f32[16,16,128]{2,1,0:T(8,128)S(1)}, u32[]{:S(2)}, u32[]{:S(2)}) collective-permute-start(f32[16,16,128]{2,1,0:T(8,128)S(1)} %get-tuple-element.78.refs_11_), channel_id=1, source_target_pairs={{0,1},{1,2},{2,3},{4,5},{5,6},{6,7},{8,9},{9,10},{10,11},{12,13},{... | collective-permute-start | bytes 393224 | tf_op jit(solution)/shard_map/ppermute | solution.py:277
  (16 other events, 171.2 us)

commit v2 on v1

--- a/solution.py
+++ b/solution.py
@@ -213,22 +213,112 @@
     return got_out[0], got_out[1], got_out[2:]
 
 
-def pick_patches(table, indices):
-    count = indices.shape[0]
-
-    def body(index_ref, source, out):
-        out[...] = source[...]
-
+def sends_of(axis):
+    index, devices = lax.axis_index(axis), lax.axis_size(axis)
+    up = ({axis: lax.rem(index + 1, devices)}, index < devices - 1, index > 0)
+    down = ({axis: lax.rem(index + devices - 1, devices)}, index > 0, index < devices - 1)
+    return up, down
+
+
+def greet(links):
+    barrier = pltpu.get_barrier_semaphore()
+    for target, sends, _ in links:
+
+        @pl.when(sends)
+        def _(target=target):
+            pl.semaphore_signal(
+                barrier, inc=1, device_id=target, device_id_type=pl.DeviceIdType.MESH
+            )
+
+    pl.semaphore_wait(barrier, sum(sends.astype(jnp.int32) for _, sends, _ in links))
+
+
+def remote(source, target, send_sem, recv_sem, link):
+    return pltpu.make_async_remote_copy(
+        src_ref=source,
+        dst_ref=target,
+        send_sem=send_sem,
+        recv_sem=recv_sem,
+        device_id=link[0],
+        device_id_type=pl.DeviceIdType.MESH,
+    )
+
+
+def finish(copies):
+    for copy, link in copies:
+        pl.when(link[2])(copy.wait_recv)
+    for copy, link in copies:
+        pl.when(link[1])(copy.wait_send)
+
+
+def exchange_kernel(west, east, south, north, *refs):
+    got, send_sem, recv_sem = refs[:4], refs[4], refs[5]
+    links = sends_of("gx") + sends_of("gy")
+    greet(links)
+    copies = []
+    for d, source in enumerate((east, west, north, south)):
+        copy = remote(source, got[d], send_sem.at[d], recv_sem.at[d], links[d])
+        pl.when(links[d][1])(copy.start)
+        copies.append((copy, links[d]))
+    finish(copies)
+
+
+def exchange(strips):
+    anywhere = pl.BlockSpec(memory_space=pl.ANY)
     return pl.pallas_call(
-        body,
-        grid_spec=pltpu.PrefetchScalarGridSpec(
-            num_scalar_prefetch=1,
-            grid=(count,),
-            in_specs=[pl.BlockSpec((1, 3, 128, 128), lambda i, ind: (ind[i], 0, 0, 0))],
-            out_specs=pl.BlockSpec((1, 3, 128, 128), lambda i, ind: (i, 0, 0, 0)),
+        exchange_kernel,
+        in_specs=[anywhere] * 4,
+        out_specs=[anywhere] * 4,
+        out_shape=[jax.ShapeDtypeStruct(strips[0].shape, jnp.float32)] * 4,
+        scratch_shapes=[pltpu.SemaphoreType.DMA((4,)), pltpu.SemaphoreType.DMA((4,))],
+        compiler_params=pltpu.CompilerParams(collective_id=0, has_side_effects=True),
+        name="exchange",
+    )(*strips)
+
+
+PIECE = 2
+
+
+def rebalance_kernel(indices, table, low, high, packed, send_sem, recv_sem):
+    links = sends_of("gx")
+    greet(links)
+    copies = []
+    for piece in range(MOVE // PIECE):
+        for d, target in enumerate((low, high)):
+            begin = piece * PIECE
+            for k in range(PIECE):
+                packed[d * MOVE + begin + k] = table[indices[d * MOVE + begin + k]]
+            n = d * (MOVE // PIECE) + piece
+            copy = remote(
+                packed.at[pl.ds(d * MOVE + begin, PIECE)],
+                target.at[pl.ds(begin, PIECE)],
+                send_sem.at[n],
+                recv_sem.at[n],
+                links[d],
+            )
+            pl.when(links[d][1])(copy.start)
+            copies.append((copy, links[d]))
+    finish(copies)
+
+
+def rebalance(table, indices):
+    anywhere = pl.BlockSpec(memory_space=pl.ANY)
+    pieces = 2 * (MOVE // PIECE)
+    patch = table.shape[1:]
+    return pl.pallas_call(
+        rebalance_kernel,
+        in_specs=[pl.BlockSpec(memory_space=pltpu.SMEM), pl.BlockSpec(memory_space=pltpu.VMEM)],
+        out_specs=[anywhere] * 2,
+        out_shape=[jax.ShapeDtypeStruct((MOVE,) + patch, jnp.float32)] * 2,
+        scratch_shapes=[
+            pltpu.VMEM((2 * MOVE,) + patch, jnp.float32),
+            pltpu.SemaphoreType.DMA((pieces,)),
+            pltpu.SemaphoreType.DMA((pieces,)),
+        ],
+        compiler_params=pltpu.CompilerParams(
+            collective_id=1, has_side_effects=True, vmem_limit_bytes=VMEM_BYTES
         ),
-        out_shape=jax.ShapeDtypeStruct((count, 3, 128, 128), jnp.float32),
-        name="pick",
+        name="rebalance",
     )(indices, table)
 
 
@@ -271,21 +361,6 @@
     return out[0], out[1], out[2], out[3:]
 
 
-def shifted(value, axis, up):
-    devices = lax.axis_size(axis)
-    pairs = [(i, i + 1) for i in range(devices - 1)]
-    return lax.ppermute(value, axis, pairs if up else [(j, i) for i, j in pairs])
-
-
-def exchange(strips):
-    return [
-        shifted(strips[1], "gx", True),
-        shifted(strips[0], "gx", False),
-        shifted(strips[3], "gy", True),
-        shifted(strips[2], "gy", False),
-    ]
-
-
 def on_device(old_state, bed, roughness, levels, sources, neighbours, face_codes, step_index):
     owned = levels.shape[0]
     capacity = old_state.shape[0]
@@ -305,9 +380,7 @@
         return jnp.sum(jnp.where(hit, theirs % capacity, 0), axis=1)
 
     sends = jnp.concatenate([to_send(device + across), to_send(device - across)])
-    picked = pick_patches(old_state, sends.astype(jnp.int32))
-    from_low = shifted(picked[:MOVE], "gx", True)
-    from_high = shifted(picked[MOVE:], "gx", False)
+    from_low, from_high = rebalance(old_state, sends.astype(jnp.int32))
 
     mine = lax.dynamic_slice_in_dim(sources, device * owned, owned)
     source_dev = mine // capacity

time: 252 us -> 271 us (1.075)
  starting transfers between devices: 89.5 us -> 0 us
  local copies, waits for them, and re-layouts: 20.2 us -> 99.4 us
  Pallas kernels: 115 us -> 164 us
  waiting for transfers between devices: 17.5 us -> 0 us
    ppermute x26 -> x0, starting transfers between devices: 89.5 us -> none  [shifted(): lax.ppermute(value, axis, pairs if up else [(j, i) for i, j in pairs])]
    unnamed x29 -> x191, local copies, waits for them, and re-layouts: 12.6 us -> 97.4 us
    pallas_call x1 -> x7, Pallas kernels: 7.19 us -> 58.5 us  [the longest x6 51.8 us: exchange(): pl.pallas_call(exchange_kernel, in_specs=[anywhere] * 4, out_specs=[anywh...]
    ppermute x26 -> x0, waiting for transfers between devices: 17.5 us -> none  [shifted(): lax.ppermute(value, axis, pairs if up else [(j, i) for i, j in pairs])]
    slice x1 -> x0, local copies, waits for them, and re-layouts: 4.03 us -> none  [on_device(): from_high = shifted(picked[MOVE:], 'gx', False)]
  transfers between devices with their start and end apart: 26 -> 0, of which waited for: 11 -> 0; matrix products, arithmetic and copies ran while one was open for 3% -> 0% of each run, Pallas kernels for 0% -> 0%
where the time goes in v2:
time: 271 us; the launch traced here: 268 us
  Pallas kernels  164 us (61%)
  local copies, waits for them, and re-layouts  99.4 us (37%)
  other arithmetic  4.37 us (2%)
    unnamed x191, local copies, waits for them, and re-layouts  97.4 us
    pallas_call x6, Pallas kernels, stage(): pl.pallas_call(functools.partial(stage_kernel, second_stage, step), grid=...  96.4 us
    pallas_call x6, Pallas kernels, exchange(): pl.pallas_call(exchange_kernel, in_specs=[anywhere] * 4, out_specs=[anywh...  51.8 us
    pallas_call x1, Pallas kernels, assemble(): pl.pallas_call(body, grid_spec=pltpu.PrefetchScalarGridSpec(num_scalar_pr...  8.88 us
    pallas_call x1, Pallas kernels, rebalance(): pl.pallas_call(rebalance_kernel, in_specs=[pl.BlockSpec(memory_space=pltp...  6.73 us

profile of v2, /device:TPU:0, one launch (start us, length us, event | category | flops | bytes accessed | tf_op | source)
XLA Modules:
  0.0 267.9 jit_solution(11549466330277022371)
XLA Ops:
  7.2 2.8 %copy-done.2 = f32[32,3,128,128]{3,2,1,0:T(8,128)S(1)} copy-done((f32[32,3,128,128]{3,2,1,0:T(8,128)S(1)}, f32[32,3,128,128]{3,2,1,0:T(8,128)}, u32[]{:S(2)}) %copy-start.2) | copy-done | bytes 6291480
  10.0 6.7 %rebalance.1 = (f32[8,3,128,128]{3,2,1,0:T(8,128)S(1)}, f32[8,3,128,128]{3,2,1,0:T(8,128)S(1)}) custom-call(s32[16]{0:T(128)S(1)} %pad_add_fusion.2.indices, f32[32,3,128,128]{3,2,1,0:T(8,128)S(1)} %copy-done.2), custom_call_target="tpu_custom_call" | custom-call | tf_op jit(solution)/shard_map/rebalance/pallas_call | solution.py:308
  16.7 8.9 %assemble.1 = (f32[16,3,128,128]{3,2,1,0:T(8,128)S(1)}, f32[16,3,128,128]{3,2,1,0:T(8,128)S(1)}, f32[16,128,128]{2,1,0:T(8,128)S(1)}, f32[16,16,128]{2,1,0:T(8,1...) custom-call(s32[4,16]{1,0:T(4,128)S(1)} %pad_add_fusion.1.picks_ref, ...), custom_call_target="tpu_custom_call" | custom-call | tf_op jit(solution)/shard_map/assemble/pallas_call | solution.py:349
  31.5 19.3 %exchange.6 = (f32[16,16,128]{2,1,0:T(8,128)}, f32[16,16,128]{2,1,0:T(8,128)}, f32[16,16,128]{2,1,0:T(8,128)}, f32[16,16,128]{2,1,0:T(8,128)}) custom-call(f32[16,16,128]{2,1,0:T(8,128)} %copy-done.55, f32[16,16,128]{2,1,0:T(8,128)} %copy-done.57, f32[16,16,128]{2,1,0:T(8,128)} %copy-done.59, f32[16,16,128]{2,1,0:T(8,128)} %copy-done.61), custom_call_target="tpu_custom_call" | custom-call | tf_op jit(solution)/shard_map/exchange/pallas_call | solution.py:268
  50.8 1.9 copy-done.6
  60.0 15.6 %stage.6 = (f32[16,3,128,128]{3,2,1,0:T(8,128)S(1)}, f32[16,3,128,128]{3,2,1,0:T(8,128)S(1)}, f32[16,16,128]{2,1,0:T(8,128)S(1)}, f32[16,16,128]{2,1,0:T(8,128)S...) custom-call(s32[4,64]{1,0:T(4,128)S(1)} %pad_add_fusion.refs_0_, f32[19]{0:T(128)S(1)} %pad_maximum_fusion.refs_1_, ...), custom_call_target="tpu_custom_call" | custom-call | tf_op jit(solution)/shard_map/stage/pallas_call | solution.py:201
  81.5 8.5 %exchange.7 = (f32[16,16,128]{2,1,0:T(8,128)}, f32[16,16,128]{2,1,0:T(8,128)}, f32[16,16,128]{2,1,0:T(8,128)}, f32[16,16,128]{2,1,0:T(8,128)}) custom-call(f32[16,16,128]{2,1,0:T(8,128)} %copy-done.39, f32[16,16,128]{2,1,0:T(8,128)} %copy-done.41, f32[16,16,128]{2,1,0:T(8,128)} %copy-done.43, f32[16,16,128]{2,1,0:T(8,128)} %copy-done.45), custom_call_target="tpu_custom_call" | custom-call | tf_op jit(solution)/shard_map/exchange/pallas_call | solution.py:268
  90.0 1.9 copy-done.13
  99.1 17.0 %stage.7 = (f32[16,3,128,128]{3,2,1,0:T(8,128)S(1)}, f32[16,3,128,128]{3,2,1,0:T(8,128)S(1)}, f32[16,16,128]{2,1,0:T(8,128)S(1)}, f32[16,16,128]{2,1,0:T(8,128)S...) custom-call(s32[4,64]{1,0:T(4,128)S(1)} %pad_add_fusion.refs_0_, f32[19]{0:T(128)S(1)} %pad_maximum_fusion.refs_1_, ...), custom_call_target="tpu_custom_call" | custom-call | tf_op jit(solution)/shard_map/stage/pallas_call | solution.py:201
  122.0 6.4 %exchange.8 = (f32[16,16,128]{2,1,0:T(8,128)}, f32[16,16,128]{2,1,0:T(8,128)}, f32[16,16,128]{2,1,0:T(8,128)}, f32[16,16,128]{2,1,0:T(8,128)}) custom-call(f32[16,16,128]{2,1,0:T(8,128)} %copy-done.23, f32[16,16,128]{2,1,0:T(8,128)} %copy-done.25, f32[16,16,128]{2,1,0:T(8,128)} %copy-done.27, f32[16,16,128]{2,1,0:T(8,128)} %copy-done.29), custom_call_target="tpu_custom_call" | custom-call | tf_op jit(solution)/shard_map/exchange/pallas_call | solution.py:268
  128.5 1.9 copy-done.4
  137.6 15.7 %stage.8 = (f32[16,3,128,128]{3,2,1,0:T(8,128)S(1)}, f32[16,3,128,128]{3,2,1,0:T(8,128)S(1)}, f32[16,16,128]{2,1,0:T(8,128)S(1)}, f32[16,16,128]{2,1,0:T(8,128)S...) custom-call(s32[4,64]{1,0:T(4,128)S(1)} %pad_add_fusion.refs_0_, f32[19]{0:T(128)S(1)} %pad_maximum_fusion.refs_1_, ...), custom_call_target="tpu_custom_call" | custom-call | tf_op jit(solution)/shard_map/stage/pallas_call | solution.py:201
  159.2 6.3 %exchange.9 = (f32[16,16,128]{2,1,0:T(8,128)}, f32[16,16,128]{2,1,0:T(8,128)}, f32[16,16,128]{2,1,0:T(8,128)}, f32[16,16,128]{2,1,0:T(8,128)}) custom-call(f32[16,16,128]{2,1,0:T(8,128)} %copy-done.47, f32[16,16,128]{2,1,0:T(8,128)} %copy-done.49, f32[16,16,128]{2,1,0:T(8,128)} %copy-done.51, f32[16,16,128]{2,1,0:T(8,128)} %copy-done.53), custom_call_target="tpu_custom_call" | custom-call | tf_op jit(solution)/shard_map/exchange/pallas_call | solution.py:268
  165.5 1.9 copy-done.16
  174.7 17.0 %stage.9 = (f32[16,3,128,128]{3,2,1,0:T(8,128)S(1)}, f32[16,3,128,128]{3,2,1,0:T(8,128)S(1)}, f32[16,16,128]{2,1,0:T(8,128)S(1)}, f32[16,16,128]{2,1,0:T(8,128)S...) custom-call(s32[4,64]{1,0:T(4,128)S(1)} %pad_add_fusion.refs_0_, f32[19]{0:T(128)S(1)} %pad_maximum_fusion.refs_1_, ...), custom_call_target="tpu_custom_call" | custom-call | tf_op jit(solution)/shard_map/stage/pallas_call | solution.py:201
  197.5 5.5 %exchange.10 = (f32[16,16,128]{2,1,0:T(8,128)}, f32[16,16,128]{2,1,0:T(8,128)}, f32[16,16,128]{2,1,0:T(8,128)}, f32[16,16,128]{2,1,0:T(8,128)}) custom-call(f32[16,16,128]{2,1,0:T(8,128)} %copy-done.31, f32[16,16,128]{2,1,0:T(8,128)} %copy-done.33, f32[16,16,128]{2,1,0:T(8,128)} %copy-done.35, f32[16,16,128]{2,1,0:T(8,128)} %copy-done.37), custom_call_target="tpu_custom_call" | custom-call | tf_op jit(solution)/shard_map/exchange/pallas_call | solution.py:268
  203.1 1.9 copy-done.8
  212.2 15.7 %stage.10 = (f32[16,3,128,128]{3,2,1,0:T(8,128)S(1)}, f32[16,3,128,128]{3,2,1,0:T(8,128)S(1)}, f32[16,16,128]{2,1,0:T(8,128)S(1)}, f32[16,16,128]{2,1,0:T(8,128)...) custom-call(s32[4,64]{1,0:T(4,128)S(1)} %pad_add_fusion.refs_0_, f32[19]{0:T(128)S(1)} %pad_maximum_fusion.refs_1_, ...), custom_call_target="tpu_custom_call" | custom-call | tf_op jit(solution)/shard_map/stage/pallas_call | solution.py:201
  229.5 1.7 copy-done.21
  233.8 5.6 %exchange.11 = (f32[16,16,128]{2,1,0:T(8,128)}, f32[16,16,128]{2,1,0:T(8,128)}, f32[16,16,128]{2,1,0:T(8,128)}, f32[16,16,128]{2,1,0:T(8,128)}) custom-call(f32[16,16,128]{2,1,0:T(8,128)} %copy-done.63, f32[16,16,128]{2,1,0:T(8,128)} %copy-done.65, f32[16,16,128]{2,1,0:T(8,128)} %copy-done.67, f32[16,16,128]{2,1,0:T(8,128)} %copy-done.69), custom_call_target="tpu_custom_call" | custom-call | tf_op jit(solution)/shard_map/exchange/pallas_call | solution.py:268
  239.4 1.9 copy-done.9
  241.3 1.9 copy-done.20
  243.2 1.9 copy-done.22
  252.3 15.5 %stage.11 = f32[16,3,128,128]{3,2,1,0:T(8,128)} custom-call(s32[4,64]{1,0:T(4,128)S(1)} %pad_add_fusion.refs_0_, f32[19]{0:T(128)S(1)} %pad_maximum_fusion.refs_1_, f32[16,3,128,128]{3,2,1,0:T(8,128)S(1)} %copy-done.20, f32[16,3,128,128]{3,2,1,0:T(8,128)S(1)} %copy-done.22, f32[16,128,128]{2,1,0:T(8,128)S(1)} %copy-done, ...), custom_call_target="tpu_custom_call" | custom-call | tf_op jit(solution)/shard_map/stage/pallas_call | solution.py:201
  (206 shorter events, 84.2 us)
Async XLA Ops:
  7.2 2.8 %copy-start.2 = (f32[32,3,128,128]{3,2,1,0:T(8,128)S(1)}, f32[32,3,128,128]{3,2,1,0:T(8,128)}, u32[]{:S(2)}) copy-start(f32[32,3,128,128]{3,2,1,0:T(8,128)} %here.1) | copy-start | bytes 18874372
  10.0 6.7 %copy-start = (f32[16,128,128]{2,1,0:T(8,128)S(1)}, f32[16,128,128]{2,1,0:T(8,128)}, u32[]{:S(2)}) copy-start(f32[16,128,128]{2,1,0:T(8,128)} %refs_4_.11) | copy-start | bytes 3145732
  16.7 34.1 %copy-start.1 = (f32[16,128,128]{2,1,0:T(8,128)S(1)}, f32[16,128,128]{2,1,0:T(8,128)}, u32[]{:S(2)}) copy-start(f32[16,128,128]{2,1,0:T(8,128)} %refs_6_.11) | copy-start | bytes 3145732
  25.6 1.7 copy-start.5
  27.3 1.6 copy-start.18
  50.8 1.9 copy-start.6
  55.4 0.9 copy-start.62
  75.6 1.7 copy-start.12
  77.2 1.6 copy-start.14
  90.0 1.9 copy-start.13
  116.1 1.7 copy-start.3
  117.8 1.6 copy-start.10
  128.5 1.9 copy-start.4
  153.3 1.7 copy-start.15
  155.0 1.6 copy-start.17
  165.5 1.9 copy-start.16
  191.6 1.7 copy-start.7
  193.3 1.6 copy-start.11
  203.1 1.9 copy-start.8
  227.9 1.6 copy-start.19
  229.5 1.7 copy-start.21
  239.4 1.9 copy-start.9
  241.3 1.9 copy-start.20
  243.2 1.9 copy-start.22
  (71 other events, 58.1 us)

commit v3 on v2

--- a/solution.py
+++ b/solution.py
@@ -12,7 +12,6 @@
 GRAVITY = 9.81
 COARSE_SPACING = 32.0
 STEP_BASE = 0.15
-VMEM_BYTES = 40 * 1024 * 1024
 OPPOSITE = (1, 0, 3, 2)
 FLIPPED = (1, 1, 2, 2)
 LOW, HIGH = 8, 136
@@ -205,7 +204,6 @@
         out_specs=out_specs,
         out_shape=out_shape,
         scratch_shapes=scratch,
-        compiler_params=pltpu.CompilerParams(vmem_limit_bytes=VMEM_BYTES),
         name="stage",
     )(*args)
     if len(got_out) == 1:
@@ -315,9 +313,7 @@
             pltpu.SemaphoreType.DMA((pieces,)),
             pltpu.SemaphoreType.DMA((pieces,)),
         ],
-        compiler_params=pltpu.CompilerParams(
-            collective_id=1, has_side_effects=True, vmem_limit_bytes=VMEM_BYTES
-        ),
+        compiler_params=pltpu.CompilerParams(collective_id=1, has_side_effects=True),
         name="rebalance",
     )(indices, table)
 
@@ -355,7 +351,6 @@
             out_specs=[each(3, 128, 128), each(3, 128, 128), each(128, 128)] + [each(16, 128)] * 4,
         ),
         out_shape=[field, field, jax.ShapeDtypeStruct(bed.shape, jnp.float32)] + [strip] * 4,
-        compiler_params=pltpu.CompilerParams(vmem_limit_bytes=VMEM_BYTES),
         name="assemble",
     )(picks, old_state, from_low, from_high, bed)
     return out[0], out[1], out[2], out[3:]

time: 271 us -> 203 us (0.75)
  local copies, waits for them, and re-layouts: 99.4 us -> 2.77 us
  Pallas kernels: 164 us -> 190 us
    unnamed x191 -> x1, local copies, waits for them, and re-layouts: 97.4 us -> 0.76 us
    pallas_call x6, Pallas kernels: 96.4 us -> 117 us  [stage(): pl.pallas_call(functools.partial(stage_kernel, second_stage, step), grid=...]
    pallas_call x1, Pallas kernels: 8.88 us -> 12.1 us  [assemble(): pl.pallas_call(body, grid_spec=pltpu.PrefetchScalarGridSpec(num_scalar_pr...]
where the time goes in v3:
time: 203 us; the launch traced here: 200 us
  Pallas kernels  190 us (94%)
  other arithmetic  6.58 us (3%)
  local copies, waits for them, and re-layouts  2.77 us (1%)
    pallas_call x6, Pallas kernels, stage(): pl.pallas_call(functools.partial(stage_kernel, second_stage, step), grid=...  117 us
    pallas_call x6, Pallas kernels, exchange(): pl.pallas_call(exchange_kernel, in_specs=[anywhere] * 4, out_specs=[anywh...  52.6 us
    pallas_call x1, Pallas kernels, assemble(): pl.pallas_call(body, grid_spec=pltpu.PrefetchScalarGridSpec(num_scalar_pr...  12.1 us
    pallas_call x1, Pallas kernels, rebalance(): pl.pallas_call(rebalance_kernel, in_specs=[pl.BlockSpec(memory_space=pltp...  9.12 us

profile of v3, /device:TPU:0, one launch (start us, length us, event | category | flops | bytes accessed | tf_op | source)
XLA Modules:
  0.0 199.9 jit_solution(17717867348486831817)
XLA Ops:
  0.0 0.7 fusion.9
  0.7 0.7 add_multiply_fusion
  1.3 0.7 pad_maximum_fusion.refs_1_
  2.0 0.8 select_bitcast_fusion.2
  2.7 0.8 fusion.11
  3.9 0.6 pad_add_fusion.2.indices
  4.7 0.8 fusion.10
  6.0 0.7 slice.7
  6.7 0.7 slice.6
  7.9 0.8 copy.20
  9.4 9.1 %rebalance.1 = (f32[8,3,128,128]{3,2,1,0:T(8,128)}, f32[8,3,128,128]{3,2,1,0:T(8,128)}) custom-call(s32[16]{0:T(128)} %pad_add_fusion.2.indices, f32[32,3,128,128]{3,2,1,0:T(8,128)} %here.1), custom_call_target="tpu_custom_call" | custom-call | tf_op jit(solution)/shard_map/rebalance/pallas_call | solution.py:306
  18.5 12.1 %assemble.1 = (f32[16,3,128,128]{3,2,1,0:T(8,128)}, f32[16,3,128,128]{3,2,1,0:T(8,128)}, f32[16,128,128]{2,1,0:T(8,128)}, f32[16,16,128]{2,1,0:T(8,128)}, f32[16...) custom-call(s32[4,16]{1,0:T(4,128)} %pad_add_fusion.1.picks_ref, f32[32,3,128,128]{3,2,1,0:T(8,128)} %here.1, ...), custom_call_target="tpu_custom_call" | custom-call | tf_op jit(solution)/shard_map/assemble/pallas_call | solution.py:345
  30.6 21.4 %exchange.6 = (f32[16,16,128]{2,1,0:T(8,128)}, f32[16,16,128]{2,1,0:T(8,128)}, f32[16,16,128]{2,1,0:T(8,128)}, f32[16,16,128]{2,1,0:T(8,128)}) custom-call(f32[16,16,128]{2,1,0:T(8,128)} %get-tuple-element.73.west.refs_7_, f32[16,16,128]{2,1,0:T(8,128)} %get-tuple-element.74.east.refs_8_, f32[16,16,128]{2,1,0:T(8,128)} %get-tuple-element.75.south.refs_9_, ...), custom_call_target="tpu_custom_call" | custom-call | tf_op jit(solution)/shard_map/exchange/pallas_call | solution.py:266
  52.0 19.0 %stage.6 = (f32[16,3,128,128]{3,2,1,0:T(8,128)}, f32[16,3,128,128]{3,2,1,0:T(8,128)}, f32[16,16,128]{2,1,0:T(8,128)}, f32[16,16,128]{2,1,0:T(8,128)}, f32[16,16,128]{2,1,0:T(8,128)}, /*index=5*/f32[16,16,128]{2,1,0:T(8,128)}) custom-call(s32[4,64]{1,0:T(4,128)} %pad_add_fusion.refs_0_, f32[19]{0:T(128)} %pad_maximum_fusion.refs_1_, ...), custom_call_target="tpu_custom_call" | custom-call | tf_op jit(solution)/shard_map/stage/pallas_call | solution.py:200
  71.0 6.5 %exchange.7 = (f32[16,16,128]{2,1,0:T(8,128)}, f32[16,16,128]{2,1,0:T(8,128)}, f32[16,16,128]{2,1,0:T(8,128)}, f32[16,16,128]{2,1,0:T(8,128)}) custom-call(f32[16,16,128]{2,1,0:T(8,128)} %get-tuple-element.83.west.refs_8_, f32[16,16,128]{2,1,0:T(8,128)} %get-tuple-element.84.east.refs_9_, f32[16,16,128]{2,1,0:T(8,128)} %get-tuple-element.85.south.refs_10_, ...), custom_call_target="tpu_custom_call" | custom-call | tf_op jit(solution)/shard_map/exchange/pallas_call | solution.py:266
  77.5 20.2 %stage.7 = (f32[16,3,128,128]{3,2,1,0:T(8,128)}, f32[16,3,128,128]{3,2,1,0:T(8,128)}, f32[16,16,128]{2,1,0:T(8,128)}, f32[16,16,128]{2,1,0:T(8,128)}, f32[16,16,128]{2,1,0:T(8,128)}, /*index=5*/f32[16,16,128]{2,1,0:T(8,128)}) custom-call(s32[4,64]{1,0:T(4,128)} %pad_add_fusion.refs_0_, f32[19]{0:T(128)} %pad_maximum_fusion.refs_1_, ...), custom_call_target="tpu_custom_call" | custom-call | tf_op jit(solution)/shard_map/stage/pallas_call | solution.py:200
  97.7 6.2 %exchange.8 = (f32[16,16,128]{2,1,0:T(8,128)}, f32[16,16,128]{2,1,0:T(8,128)}, f32[16,16,128]{2,1,0:T(8,128)}, f32[16,16,128]{2,1,0:T(8,128)}) custom-call(f32[16,16,128]{2,1,0:T(8,128)} %get-tuple-element.93.west.refs_7_, f32[16,16,128]{2,1,0:T(8,128)} %get-tuple-element.94.east.refs_8_, f32[16,16,128]{2,1,0:T(8,128)} %get-tuple-element.95.south.refs_9_, ...), custom_call_target="tpu_custom_call" | custom-call | tf_op jit(solution)/shard_map/exchange/pallas_call | solution.py:266
  103.8 19.0 %stage.8 = (f32[16,3,128,128]{3,2,1,0:T(8,128)}, f32[16,3,128,128]{3,2,1,0:T(8,128)}, f32[16,16,128]{2,1,0:T(8,128)}, f32[16,16,128]{2,1,0:T(8,128)}, f32[16,16,128]{2,1,0:T(8,128)}, /*index=5*/f32[16,16,128]{2,1,0:T(8,128)}) custom-call(s32[4,64]{1,0:T(4,128)} %pad_add_fusion.refs_0_, f32[19]{0:T(128)} %pad_maximum_fusion.refs_1_, ...), custom_call_target="tpu_custom_call" | custom-call | tf_op jit(solution)/shard_map/stage/pallas_call | solution.py:200
  122.9 7.1 %exchange.9 = (f32[16,16,128]{2,1,0:T(8,128)}, f32[16,16,128]{2,1,0:T(8,128)}, f32[16,16,128]{2,1,0:T(8,128)}, f32[16,16,128]{2,1,0:T(8,128)}) custom-call(f32[16,16,128]{2,1,0:T(8,128)} %get-tuple-element.103.west.refs_8_, f32[16,16,128]{2,1,0:T(8,128)} %get-tuple-element.104.east.refs_9_, f32[16,16,128]{2,1,0:T(8,128)} %get-tuple-element.105.south.refs_10_, ...), custom_call_target="tpu_custom_call" | custom-call | tf_op jit(solution)/shard_map/exchange/pallas_call | solution.py:266
  130.0 20.2 %stage.9 = (f32[16,3,128,128]{3,2,1,0:T(8,128)}, f32[16,3,128,128]{3,2,1,0:T(8,128)}, f32[16,16,128]{2,1,0:T(8,128)}, f32[16,16,128]{2,1,0:T(8,128)}, f32[16,16,128]{2,1,0:T(8,128)}, /*index=5*/f32[16,16,128]{2,1,0:T(8,128)}) custom-call(s32[4,64]{1,0:T(4,128)} %pad_add_fusion.refs_0_, f32[19]{0:T(128)} %pad_maximum_fusion.refs_1_, ...), custom_call_target="tpu_custom_call" | custom-call | tf_op jit(solution)/shard_map/stage/pallas_call | solution.py:200
  150.1 6.0 %exchange.10 = (f32[16,16,128]{2,1,0:T(8,128)}, f32[16,16,128]{2,1,0:T(8,128)}, f32[16,16,128]{2,1,0:T(8,128)}, f32[16,16,128]{2,1,0:T(8,128)}) custom-call(f32[16,16,128]{2,1,0:T(8,128)} %get-tuple-element.113.west.refs_7_, f32[16,16,128]{2,1,0:T(8,128)} %get-tuple-element.114.east.refs_8_, f32[16,16,128]{2,1,0:T(8,128)} %get-tuple-element.115.south.refs_9_, ...), custom_call_target="tpu_custom_call" | custom-call | tf_op jit(solution)/shard_map/exchange/pallas_call | solution.py:266
  156.1 19.0 %stage.10 = (f32[16,3,128,128]{3,2,1,0:T(8,128)}, f32[16,3,128,128]{3,2,1,0:T(8,128)}, f32[16,16,128]{2,1,0:T(8,128)}, f32[16,16,128]{2,1,0:T(8,128)}, f32[16,16,128]{2,1,0:T(8,128)}, /*index=5*/f32[16,16,128]{2,1,0:T(8,128)}) custom-call(s32[4,64]{1,0:T(4,128)} %pad_add_fusion.refs_0_, f32[19]{0:T(128)} %pad_maximum_fusion.refs_1_, ...), custom_call_target="tpu_custom_call" | custom-call | tf_op jit(solution)/shard_map/stage/pallas_call | solution.py:200
  175.2 5.5 %exchange.11 = (f32[16,16,128]{2,1,0:T(8,128)}, f32[16,16,128]{2,1,0:T(8,128)}, f32[16,16,128]{2,1,0:T(8,128)}, f32[16,16,128]{2,1,0:T(8,128)}) custom-call(f32[16,16,128]{2,1,0:T(8,128)} %get-tuple-element.123.west.refs_8_, f32[16,16,128]{2,1,0:T(8,128)} %get-tuple-element.124.east.refs_9_, f32[16,16,128]{2,1,0:T(8,128)} %get-tuple-element.125.south.refs_10_, ...), custom_call_target="tpu_custom_call" | custom-call | tf_op jit(solution)/shard_map/exchange/pallas_call | solution.py:266
  180.7 19.2 %stage.11 = f32[16,3,128,128]{3,2,1,0:T(8,128)} custom-call(s32[4,64]{1,0:T(4,128)} %pad_add_fusion.refs_0_, f32[19]{0:T(128)} %pad_maximum_fusion.refs_1_, f32[16,3,128,128]{3,2,1,0:T(8,128)} %get-tuple-element.121.refs_2_, f32[16,3,128,128]{3,2,1,0:T(8,128)} %get-tuple-element.122.refs_3_, f32[16,128,128]{2,1,0:T(8,128)} %refs_4_.11, ...), custom_call_target="tpu_custom_call" | custom-call | tf_op jit(solution)/shard_map/stage/pallas_call | solution.py:200
  (16 shorter events, 2.3 us)

commit v4 on v3

--- a/solution.py
+++ b/solution.py
@@ -73,10 +73,10 @@
     low = lane < 64
     for f in range(4):
         opp = OPPOSITE[f]
-        first = ints[0, 4 * patch + f]
-        second = ints[1, 4 * patch + f]
-        far = ints[2, 4 * patch + f] == 1
-        code = ints[3, 4 * patch + f]
+        first = ints[patch, 2 * f]
+        second = ints[patch, 2 * f + 1]
+        far = ints[patch, 8 + 2 * f] == 1
+        code = ints[patch, 16 + f]
         a = jnp.where(far, got[f][first], own[opp][first])
         b = jnp.where(far, got[f][second], own[opp][second])
         index = jnp.where(
@@ -363,41 +363,34 @@
     device = lax.axis_index("gx") * across + lax.axis_index("gy")
     slots = jnp.arange(MOVE, dtype=jnp.int32)
 
-    def ranks(mask):
-        count = jnp.arange(owned)
-        before = count[:, None] > count[None, :]
-        return jnp.sum(jnp.where(before & mask[None, :], 1, 0), axis=1)
-
-    def to_send(target):
-        theirs = lax.dynamic_slice_in_dim(sources, target * owned, owned)
-        mask = theirs // capacity == device
-        hit = mask[None, :] & (ranks(mask)[None, :] == slots[:, None])
-        return jnp.sum(jnp.where(hit, theirs % capacity, 0), axis=1)
-
-    sends = jnp.concatenate([to_send(device + across), to_send(device - across)])
+    def listed(target):
+        return lax.dynamic_slice_in_dim(sources, target * owned, owned)
+
+    mine = listed(device)
+    lists = jnp.stack([listed(device + across), listed(device - across), mine, mine])
+    holders = jnp.stack([device, device, device - across, device + across])
+    masks = lists // capacity == holders[:, None]
+    count = jnp.arange(owned)
+    before = (count[:, None] > count[None, :])[None]
+    ranks = jnp.sum(jnp.where(before & masks[:, None, :], 1, 0), axis=2)
+    hits = masks[:2, None, :] & (ranks[:2, None, :] == slots[None, :, None])
+    sends = jnp.sum(jnp.where(hits, lists[:2, None, :] % capacity, 0), axis=2).reshape(-1)
     from_low, from_high = rebalance(old_state, sends.astype(jnp.int32))
 
-    mine = lax.dynamic_slice_in_dim(sources, device * owned, owned)
-    source_dev = mine // capacity
-    is_low = source_dev == device - across
-    is_high = source_dev == device + across
+    is_low, is_high = masks[2], masks[3]
     picks = jnp.stack(
         [
             jnp.where(is_low, 0, jnp.where(is_high, 2, 1)),
             jnp.where(is_low | is_high, 0, mine % capacity),
-            jnp.where(is_low, jnp.minimum(ranks(is_low), MOVE - 1), 0),
-            jnp.where(is_high, jnp.minimum(ranks(is_high), MOVE - 1), 0),
+            jnp.where(is_low, jnp.minimum(ranks[2], MOVE - 1), 0),
+            jnp.where(is_high, jnp.minimum(ranks[3], MOVE - 1), 0),
         ]
     ).astype(jnp.int32)
     state, state_t, bed_t, strips = assemble(picks, old_state, from_low, from_high, bed)
 
-    first = jnp.maximum(neighbours[:, 0::2], 0)
-    second = jnp.maximum(neighbours[:, 1::2], 0)
-    far = jnp.where(first // owned != device, 1, 0)
-    ints = jnp.stack(
-        [(first % owned).reshape(-1), (second % owned).reshape(-1), far.reshape(-1),
-         face_codes.reshape(-1)]
-    ).astype(jnp.int32)
+    named = jnp.maximum(neighbours, 0)
+    far = jnp.where(named // owned != device, 1, 0)
+    ints = jnp.concatenate([named % owned, far, face_codes], axis=1).astype(jnp.int32)
     spacing = jnp.where(
         levels == 0, COARSE_SPACING, jnp.where(levels == 1, COARSE_SPACING / 2, COARSE_SPACING / 4)
     ).astype(jnp.float32)

time: 203 us -> 201 us (level)
  other arithmetic: 6.58 us -> 4.51 us
where the time goes in v4:
time: 201 us; the launch traced here: 198 us
  Pallas kernels  190 us (95%)
  other arithmetic  4.51 us (2%)
  local copies, waits for them, and re-layouts  3.01 us (1%)
    pallas_call x6, Pallas kernels, stage(): pl.pallas_call(functools.partial(stage_kernel, second_stage, step), grid=...  117 us
    pallas_call x6, Pallas kernels, exchange(): pl.pallas_call(exchange_kernel, in_specs=[anywhere] * 4, out_specs=[anywh...  52.4 us
    pallas_call x1, Pallas kernels, assemble(): pl.pallas_call(body, grid_spec=pltpu.PrefetchScalarGridSpec(num_scalar_pr...  12.2 us
    pallas_call x1, Pallas kernels, rebalance(): pl.pallas_call(rebalance_kernel, in_specs=[pl.BlockSpec(memory_space=pltp...  9.12 us

profile of v4, /device:TPU:0, one launch (start us, length us, event | category | flops | bytes accessed | tf_op | source)
XLA Modules:
  0.0 197.9 jit_solution(17545646318716577752)
XLA Ops:
  0.0 0.7 fusion.8
  0.7 0.7 add_multiply_fusion
  1.3 0.7 pad_maximum_fusion.refs_1_
  2.1 0.9 dynamic-slice_bitcast_fusion.1
  3.0 0.8 fusion.10
  4.1 0.6 reshape.155.indices
  4.7 0.6 pad_add_fusion.2.picks_ref
  5.3 0.8 copy.11
  6.1 0.8 copy.12
  6.9 0.7 pad_add_fusion.refs_0_
  7.5 9.1 %rebalance.1 = (f32[8,3,128,128]{3,2,1,0:T(8,128)}, f32[8,3,128,128]{3,2,1,0:T(8,128)}) custom-call(s32[16]{0:T(128)} %reshape.155.indices, f32[32,3,128,128]{3,2,1,0:T(8,128)} %here.1), custom_call_target="tpu_custom_call" | custom-call | tf_op jit(solution)/shard_map/rebalance/pallas_call | solution.py:306
  16.7 12.2 %assemble.1 = (f32[16,3,128,128]{3,2,1,0:T(8,128)}, f32[16,3,128,128]{3,2,1,0:T(8,128)}, f32[16,128,128]{2,1,0:T(8,128)}, f32[16,16,128]{2,1,0:T(8,128)}, f32[16...) custom-call(s32[4,16]{1,0:T(4,128)} %pad_add_fusion.2.picks_ref, f32[32,3,128,128]{3,2,1,0:T(8,128)} %here.1, ...), custom_call_target="tpu_custom_call" | custom-call | tf_op jit(solution)/shard_map/assemble/pallas_call | solution.py:345
  28.9 21.2 %exchange.6 = (f32[16,16,128]{2,1,0:T(8,128)}, f32[16,16,128]{2,1,0:T(8,128)}, f32[16,16,128]{2,1,0:T(8,128)}, f32[16,16,128]{2,1,0:T(8,128)}) custom-call(f32[16,16,128]{2,1,0:T(8,128)} %get-tuple-element.73.west.refs_7_, f32[16,16,128]{2,1,0:T(8,128)} %get-tuple-element.74.east.refs_8_, f32[16,16,128]{2,1,0:T(8,128)} %get-tuple-element.75.south.refs_9_, ...), custom_call_target="tpu_custom_call" | custom-call | tf_op jit(solution)/shard_map/exchange/pallas_call | solution.py:266
  50.2 19.1 %stage.6 = (f32[16,3,128,128]{3,2,1,0:T(8,128)}, f32[16,3,128,128]{3,2,1,0:T(8,128)}, f32[16,16,128]{2,1,0:T(8,128)}, f32[16,16,128]{2,1,0:T(8,128)}, f32[16,16,128]{2,1,0:T(8,128)}, /*index=5*/f32[16,16,128]{2,1,0:T(8,128)}) custom-call(s32[16,20]{1,0:T(8,128)} %pad_add_fusion.refs_0_, f32[19]{0:T(128)} %pad_maximum_fusion.refs_1_, ...), custom_call_target="tpu_custom_call" | custom-call | tf_op jit(solution)/shard_map/stage/pallas_call | solution.py:200
  69.3 6.7 %exchange.7 = (f32[16,16,128]{2,1,0:T(8,128)}, f32[16,16,128]{2,1,0:T(8,128)}, f32[16,16,128]{2,1,0:T(8,128)}, f32[16,16,128]{2,1,0:T(8,128)}) custom-call(f32[16,16,128]{2,1,0:T(8,128)} %get-tuple-element.83.west.refs_8_, f32[16,16,128]{2,1,0:T(8,128)} %get-tuple-element.84.east.refs_9_, f32[16,16,128]{2,1,0:T(8,128)} %get-tuple-element.85.south.refs_10_, ...), custom_call_target="tpu_custom_call" | custom-call | tf_op jit(solution)/shard_map/exchange/pallas_call | solution.py:266
  76.0 20.1 %stage.7 = (f32[16,3,128,128]{3,2,1,0:T(8,128)}, f32[16,3,128,128]{3,2,1,0:T(8,128)}, f32[16,16,128]{2,1,0:T(8,128)}, f32[16,16,128]{2,1,0:T(8,128)}, f32[16,16,128]{2,1,0:T(8,128)}, /*index=5*/f32[16,16,128]{2,1,0:T(8,128)}) custom-call(s32[16,20]{1,0:T(8,128)} %pad_add_fusion.refs_0_, f32[19]{0:T(128)} %pad_maximum_fusion.refs_1_, ...), custom_call_target="tpu_custom_call" | custom-call | tf_op jit(solution)/shard_map/stage/pallas_call | solution.py:200
  96.0 6.4 %exchange.8 = (f32[16,16,128]{2,1,0:T(8,128)}, f32[16,16,128]{2,1,0:T(8,128)}, f32[16,16,128]{2,1,0:T(8,128)}, f32[16,16,128]{2,1,0:T(8,128)}) custom-call(f32[16,16,128]{2,1,0:T(8,128)} %get-tuple-element.93.west.refs_7_, f32[16,16,128]{2,1,0:T(8,128)} %get-tuple-element.94.east.refs_8_, f32[16,16,128]{2,1,0:T(8,128)} %get-tuple-element.95.south.refs_9_, ...), custom_call_target="tpu_custom_call" | custom-call | tf_op jit(solution)/shard_map/exchange/pallas_call | solution.py:266
  102.4 19.1 %stage.8 = (f32[16,3,128,128]{3,2,1,0:T(8,128)}, f32[16,3,128,128]{3,2,1,0:T(8,128)}, f32[16,16,128]{2,1,0:T(8,128)}, f32[16,16,128]{2,1,0:T(8,128)}, f32[16,16,128]{2,1,0:T(8,128)}, /*index=5*/f32[16,16,128]{2,1,0:T(8,128)}) custom-call(s32[16,20]{1,0:T(8,128)} %pad_add_fusion.refs_0_, f32[19]{0:T(128)} %pad_maximum_fusion.refs_1_, ...), custom_call_target="tpu_custom_call" | custom-call | tf_op jit(solution)/shard_map/stage/pallas_call | solution.py:200
  121.5 6.7 %exchange.9 = (f32[16,16,128]{2,1,0:T(8,128)}, f32[16,16,128]{2,1,0:T(8,128)}, f32[16,16,128]{2,1,0:T(8,128)}, f32[16,16,128]{2,1,0:T(8,128)}) custom-call(f32[16,16,128]{2,1,0:T(8,128)} %get-tuple-element.103.west.refs_8_, f32[16,16,128]{2,1,0:T(8,128)} %get-tuple-element.104.east.refs_9_, f32[16,16,128]{2,1,0:T(8,128)} %get-tuple-element.105.south.refs_10_, ...), custom_call_target="tpu_custom_call" | custom-call | tf_op jit(solution)/shard_map/exchange/pallas_call | solution.py:266
  128.2 20.1 %stage.9 = (f32[16,3,128,128]{3,2,1,0:T(8,128)}, f32[16,3,128,128]{3,2,1,0:T(8,128)}, f32[16,16,128]{2,1,0:T(8,128)}, f32[16,16,128]{2,1,0:T(8,128)}, f32[16,16,128]{2,1,0:T(8,128)}, /*index=5*/f32[16,16,128]{2,1,0:T(8,128)}) custom-call(s32[16,20]{1,0:T(8,128)} %pad_add_fusion.refs_0_, f32[19]{0:T(128)} %pad_maximum_fusion.refs_1_, ...), custom_call_target="tpu_custom_call" | custom-call | tf_op jit(solution)/shard_map/stage/pallas_call | solution.py:200
  148.3 5.9 %exchange.10 = (f32[16,16,128]{2,1,0:T(8,128)}, f32[16,16,128]{2,1,0:T(8,128)}, f32[16,16,128]{2,1,0:T(8,128)}, f32[16,16,128]{2,1,0:T(8,128)}) custom-call(f32[16,16,128]{2,1,0:T(8,128)} %get-tuple-element.113.west.refs_7_, f32[16,16,128]{2,1,0:T(8,128)} %get-tuple-element.114.east.refs_8_, f32[16,16,128]{2,1,0:T(8,128)} %get-tuple-element.115.south.refs_9_, ...), custom_call_target="tpu_custom_call" | custom-call | tf_op jit(solution)/shard_map/exchange/pallas_call | solution.py:266
  154.2 19.1 %stage.10 = (f32[16,3,128,128]{3,2,1,0:T(8,128)}, f32[16,3,128,128]{3,2,1,0:T(8,128)}, f32[16,16,128]{2,1,0:T(8,128)}, f32[16,16,128]{2,1,0:T(8,128)}, f32[16,16,128]{2,1,0:T(8,128)}, /*index=5*/f32[16,16,128]{2,1,0:T(8,128)}) custom-call(s32[16,20]{1,0:T(8,128)} %pad_add_fusion.refs_0_, f32[19]{0:T(128)} %pad_maximum_fusion.refs_1_, ...), custom_call_target="tpu_custom_call" | custom-call | tf_op jit(solution)/shard_map/stage/pallas_call | solution.py:200
  173.3 5.4 %exchange.11 = (f32[16,16,128]{2,1,0:T(8,128)}, f32[16,16,128]{2,1,0:T(8,128)}, f32[16,16,128]{2,1,0:T(8,128)}, f32[16,16,128]{2,1,0:T(8,128)}) custom-call(f32[16,16,128]{2,1,0:T(8,128)} %get-tuple-element.123.west.refs_8_, f32[16,16,128]{2,1,0:T(8,128)} %get-tuple-element.124.east.refs_9_, f32[16,16,128]{2,1,0:T(8,128)} %get-tuple-element.125.south.refs_10_, ...), custom_call_target="tpu_custom_call" | custom-call | tf_op jit(solution)/shard_map/exchange/pallas_call | solution.py:266
  178.7 19.1 %stage.11 = f32[16,3,128,128]{3,2,1,0:T(8,128)} custom-call(s32[16,20]{1,0:T(8,128)} %pad_add_fusion.refs_0_, f32[19]{0:T(128)} %pad_maximum_fusion.refs_1_, f32[16,3,128,128]{3,2,1,0:T(8,128)} %get-tuple-element.121.refs_2_, f32[16,3,128,128]{3,2,1,0:T(8,128)} %get-tuple-element.122.refs_3_, f32[16,128,128]{2,1,0:T(8,128)} %refs_4_.11, ...), custom_call_target="tpu_custom_call" | custom-call | tf_op jit(solution)/shard_map/stage/pallas_call | solution.py:200
  (9 shorter events, 0.5 us)
